TPU v7x, 32 devices: a whole 2x2x4 slice. The times are simulated.
32 devices in a mesh: dp: 4 (over x, core), seq: 8 (over z, y).
Axes of the slice: x: 2, y: 2, z: 4, core: 2. Of those that a mesh axis runs over, the one named last changes fastest.
Arguments:
- tokens: bfloat16 [8192, 1536], P(('dp', 'seq')), may hold values from -6 to 6
- lengths: int32 [4, 8], P('dp'), may hold values from 1 to 1024, 1920 in all within a row
- cotangent: bfloat16 [8192, 1536], P(('dp', 'seq')), may hold values from -6 to 6
- gain_attn: bfloat16 [1536], P('seq'), may hold values from 0.25 to 1.75
- w_query: bfloat16 [1536, 1536], P('seq'), may hold values from -0.15625 to 0.15625
- w_key: bfloat16 [1536, 768], P('seq'), may hold values from -0.15625 to 0.15625
- w_value: bfloat16 [1536, 768], P('seq'), may hold values from -0.15625 to 0.15625
- w_out: bfloat16 [1536, 1536], P('seq'), may hold values from -0.625 to 0.625
- gain_mlp: bfloat16 [1536], P('seq'), may hold values from 0.25 to 1.75
- w_gate: bfloat16 [1536, 4096], P('seq'), may hold values from -0.15625 to 0.15625
- w_up: bfloat16 [1536, 4096], P('seq'), may hold values from -0.15625 to 0.15625
- w_down: bfloat16 [4096, 1536], P('seq'), may hold values from -0.09375 to 0.09375
Outputs:
- output: bfloat16 [8192, 1536], P(('dp', 'seq'))
- grad_tokens: float32 [8192, 1536], P(('dp', 'seq'))
- grad_gain_attn: float32 [1536], P('seq')
- grad_query: float32 [1536, 1536], P('seq')
- grad_key: float32 [1536, 768], P('seq')
- grad_value: float32 [1536, 768], P('seq')
- grad_out: float32 [1536, 1536], P('seq')
- grad_gain_mlp: float32 [1536], P('seq')
- grad_gate: float32 [1536, 4096], P('seq')
- grad_up: float32 [1536, 4096], P('seq')
- grad_down: float32 [4096, 1536], P('seq')
Inputs may be any that keep to these rules, and one draw needn't show every extreme that they name: Each group's lengths sum to 1920; the last 128 tokens of a group are padding; one length equals 1024.
All inputs are finite; a program needn't handle non-finite values.
Results may differ from a plain program's by a relative error of at most 0.017.
Values may be sent and summed in bfloat16 or wider, within the bound.
No kernel may reach another device: no remote copies, remote signals or barrier semaphores. Data moves between devices by JAX's collectives and lax.ppermute only.
A program may use at most 320 MiB of HBM per device.

v0:
```python
import functools
import math

import jax
import jax.numpy as jnp
from jax import lax
from jax.experimental import pallas as pl
from jax.experimental.pallas import tpu as pltpu
from jax.sharding import PartitionSpec as P

HEADS = 16
KV_HEADS = 8
HEAD = 96
WINDOW = 512


EPS = 1e-05
THETA = 100000.0
BOTH = ("dp", "seq")
BF = jnp.bfloat16
F32 = jnp.float32


def send(block, target):
    n_dp, n_seq = lax.axis_size("dp"), lax.axis_size("seq")
    route = []
    for d in range(n_dp):
        for s in range(n_seq):
            to = target(d, s)
            if to is not None and 0 <= to[1] < n_seq:
                route.append((d * n_seq + s, to[0] * n_seq + to[1]))
    return lax.ppermute(block, BOTH, route)


def after(value, *others):
    return lax.optimization_barrier((value,) + others)[0]


def across_core(d, s):
    return (d ^ 1, s)


def across_x(d, s):
    return (d ^ 2, s)


def across_y(d, s):
    return (d, s ^ 1)


def gather_plane(block, *meanwhile, for_y=None, came=None):
    half = block.shape[0] // 2
    from_x, from_y = came or (
        send(block, across_x),
        send(block if for_y is None else for_y, across_y),
    )
    if meanwhile:
        from_x, from_y = lax.optimization_barrier((from_x, from_y, *meanwhile))[:2]
    first = send(from_x[:half], across_y)
    second = send(from_y[half:], across_x)
    return [block, from_y, from_x, first, second]


def plus(a, b):
    return (a.astype(F32) + b.astype(F32)).astype(BF)


def scatter_plane(near, far, *meanwhile, at_first=()):
    own, own_y = near
    far, far_a, far_b = far
    half = far_a.shape[0]
    first = send(far_a, across_y)
    second = send(far_b, across_x)
    if at_first:
        first, second = lax.optimization_barrier((first, second, *at_first))[:2]

    far = jnp.concatenate([plus(far[:half], first), far[half:]], axis=0)
    own_y = jnp.concatenate([own_y[:half], plus(own_y[half:], second)], axis=0)
    from_x, from_y = send(far, across_x), send(own_y, across_y)
    if meanwhile:
        from_x, from_y = lax.optimization_barrier((from_x, from_y, *meanwhile))[:2]
    return own.astype(F32) + from_x.astype(F32) + from_y.astype(F32)


def with_core(block):
    return [block, send(block, across_core)]


def sum_core(mine, other):
    return (mine.astype(F32) + send(other.astype(BF), across_core).astype(F32)).astype(BF)


def across_z(k):
    return lambda d, s: (d, s ^ (2 * k))


def along_z(blocks):
    n_seq = lax.axis_size("seq")
    lines = [list(range(y, n_seq, 2)) for y in range(2)]
    return lax.all_to_all(blocks, "seq", 0, 0, axis_index_groups=lines)


def gather_z(block):
    return along_z(jnp.broadcast_to(block[None], (lax.axis_size("seq") // 2,) + block.shape))


def scatter_z(blocks):
    return jnp.sum(along_z(blocks).astype(F32), axis=0)


def pair_y(mine, other):
    y = lax.axis_index("seq") % 2
    return jnp.stack([jnp.where(y == 0, mine, other), jnp.where(y == 0, other, mine)])


def turned(d, s):
    return (s // 2, 2 * d + s % 2)


def fold(rows, wide):
    count, columns = rows.shape
    whole = columns // wide
    parts = [rows[:, i * wide : (i + 1) * wide] for i in range(whole)]
    rest = rows[:, whole * wide :]
    if rest.shape[1]:
        times = wide // rest.shape[1]
        step = count // times
        parts.append(
            jnp.concatenate([rest[i * step : (i + 1) * step] for i in range(times)], axis=1)
        )
    return jnp.concatenate(parts, axis=0)


def unfold(folded, columns):
    total, wide = folded.shape
    count = total * wide // columns
    whole = columns // wide
    parts = [folded[i * count : (i + 1) * count] for i in range(whole)]
    if columns % wide:
        rest, narrow = folded[whole * count :], columns % wide
        parts.append(
            jnp.concatenate(
                [rest[:, i * narrow : (i + 1) * narrow] for i in range(wide // narrow)], axis=0
            )
        )
    return jnp.concatenate(parts, axis=1)


def gather_dp(block, *meanwhile):
    core = send(block, across_core)
    far = send(block, across_x)
    if meanwhile:
        far = lax.optimization_barrier((far, *meanwhile))[0]
    return [block, core, far, send(far, across_core)]


def order_dp(blocks):
    d = lax.axis_index("dp")
    pairs = [
        (jnp.where(d % 2 == 0, a, b), jnp.where(d % 2 == 0, b, a))
        for a, b in (blocks[:2], blocks[2:])
    ]
    low, high = pairs
    return [jnp.where(d < 2, a, b) for a, b in zip(low, high)] + [
        jnp.where(d < 2, b, a) for a, b in zip(low, high)
    ]


def rope_tables(position):
    lane = jnp.arange(128, dtype=jnp.float32) % (HEAD // 2)
    angles = position.astype(jnp.float32)[..., None] * THETA ** (-2.0 * lane / HEAD)
    return jnp.cos(angles), jnp.sin(angles)


SCALE = 0.3
VMEM_BYTES = 60 * 1024 * 1024


def call(kernel, out_shape, flops, moved, **rest):
    return pl.pallas_call(
        kernel,
        out_shape=out_shape,
        compiler_params=pltpu.CompilerParams(vmem_limit_bytes=VMEM_BYTES),
        cost_estimate=pl.CostEstimate(flops=int(flops * SCALE), bytes_accessed=int(moved * SCALE), transcendentals=0),
        **rest,
    )


def shaped(shape, dtype):
    return jax.ShapeDtypeStruct(shape, dtype)


def iota(shape, axis):
    return lax.broadcasted_iota(jnp.int32, shape, axis)


def dot(a, b):
    return jnp.dot(a, b, preferred_element_type=F32)


def dot_nt(a, b):
    return lax.dot_general(a, b, (((1,), (1,)), ((), ())), preferred_element_type=F32)


def dot_tn(a, b):
    return lax.dot_general(a, b, (((0,), (0,)), ((), ())), preferred_element_type=F32)


def spread(packed, heads, base):
    row, column = iota((packed, heads * 128), 0), iota((packed, heads * 128), 1)
    lane = column % 128
    hit = (row == base + HEAD * (column // 128) + lane) & (lane < HEAD)
    return jnp.where(hit, 1.0, 0.0).astype(BF)


def pack(packed, heads, base):
    column, row = iota((heads * 128, packed), 0), iota((heads * 128, packed), 1)
    lane = column % 128
    hit = (row == base + HEAD * (column // 128) + lane) & (lane < HEAD)
    return jnp.where(hit, 1.0, 0.0).astype(BF)


def on_heads(table, heads, packed):
    row, column = iota((128, packed), 0), iota((128, packed), 1)
    place = jnp.where((row == column % HEAD) & (column < heads * HEAD), 1.0, 0.0).astype(BF)
    high = table.astype(BF)
    rest = table - high.astype(F32)
    middle = rest.astype(BF)
    low = (rest - middle.astype(F32)).astype(BF)
    return dot(high, place) + dot(middle, place) + dot(low, place)


def qkv_kernel(*refs):
    parts, refs = refs[:-8], refs[-8:]
    gain, cosine, sine, w_own, w_core, normed, qkv, halo = refs
    tokens, lanes = halo.shape
    x = jnp.concatenate([part[...] for part in parts], axis=0).astype(F32)
    inverse = lax.rsqrt(jnp.mean(x * x, axis=-1, keepdims=True) + EPS)
    low = (x * inverse * gain[...]).astype(BF)
    normed[...] = low
    lane = iota((tokens, lanes), 1)
    first = lane % HEAD < HEAD // 2
    cos_all = on_heads(cosine[...], 3, lanes) + jnp.where(lane >= 3 * HEAD, 1.0, 0.0)
    sin_all = on_heads(sine[...], 3, lanes)
    turned = []
    size = normed.shape[1] // w_own.shape[0]
    for w in (w_own, w_core):
        raw = sum(dot(low[:, z * size : (z + 1) * size], w[z, :size, :]) for z in range(w.shape[0]))
        half = jnp.where(
            first, -pltpu.roll(raw, lanes - HEAD // 2, 1), pltpu.roll(raw, HEAD // 2, 1)
        )
        turned.append(raw * cos_all + half * sin_all)
    qkv[0] = turned[0].astype(BF)
    qkv[1] = turned[1].astype(BF)
    halo[...] = jnp.where(
        lane < lanes // 2, pltpu.roll(turned[1], lanes // 2, 1), turned[0]
    ).astype(BF)


def project(group, parts, gain, cosine, sine, w_own, w_core):
    tokens = sum(part.shape[0] for part in parts)
    width, lanes = gain.shape[1], w_own.shape[2]

    def whole(array):
        return pl.BlockSpec(array.shape, lambda i: (0,) * array.ndim)

    table = pl.BlockSpec((tokens, 128), lambda i: (group, 0))
    outs = [shaped((tokens, width), BF), shaped((2, tokens, lanes), BF), shaped((tokens, lanes), BF)]
    return call(
        qkv_kernel,
        outs,
        flops=4 * tokens * width * lanes,
        moved=6 * 10**6,
        grid=(1,),
        in_specs=[whole(part) for part in parts] + [whole(gain), table, table, whole(w_own), whole(w_core)],
        out_specs=[whole(out) for out in outs],
    )(*parts, gain, cosine, sine, w_own, w_core)


def visible(seg_query, seg_key, a, rows):
    shape = (rows, 3 * rows)
    row, column = iota(shape, 0), iota(shape, 1)
    same = seg_query[0, a] == jnp.concatenate([seg_key[0, a + i] for i in range(3)], axis=1)
    allowed = (column > row) & (column <= row + 2 * rows) & same
    return jnp.concatenate([allowed, allowed], axis=0)


def heads_of(y, slot, qkv, halo, rows):
    lanes = qkv.shape[-1]

    def at(a):
        return pl.ds(pl.multiple_of((a ^ y) * rows, rows), rows)

    before = spread(lanes, 2, (1 - slot) * (lanes // 2))
    here = spread(lanes, 4, 0)
    local = [dot(qkv[0, at(a), :], here).astype(BF) for a in range(2)]
    key_value = [dot(halo[at(a), :], before).astype(BF) for a in range(2)]
    key_value += [part[:, 256:] for part in local]
    query = [jnp.concatenate([part[:, :128], part[:, 128:256]], axis=0) for part in local]
    return at, query, key_value


def padded_out(w_out):
    rows = w_out.shape[1]
    return dot(pack(rows, 2, 0), w_out[0]).astype(BF)


def attend_kernel(y_ref, qkv, halo, seg_query, seg_key, w_out, *refs):
    *partial, context, logsum, total = refs
    slot = pl.program_id(0)
    rows = qkv.shape[1] // 2
    at, query, key_value = heads_of(y_ref[0], slot, qkv, halo, rows)
    w = padded_out(w_out)
    for a in range(2):
        kv = jnp.concatenate(key_value[a : a + 3], axis=0)
        scores = dot_nt(query[a], kv[:, :128]) * (1.0 / math.sqrt(HEAD))
        scores = jnp.where(visible(seg_query, seg_key, a, rows), scores, -1e30)
        peak = jnp.max(scores, axis=-1, keepdims=True)
        exponent = jnp.exp(scores - peak)
        row_total = jnp.sum(exponent, axis=-1, keepdims=True)
        probs = (exponent * (1.0 / row_total)).astype(BF)
        logsum[0, a] = peak + jnp.log(row_total)
        seen = dot(probs, kv[:, 128:]).astype(BF)
        seen = jnp.concatenate([seen[:rows], seen[rows:]], axis=1)
        context[0, at(a), :] = seen
        product = dot(seen, w)

        @pl.when(slot == 0)
        def _():
            total[at(a), :] = product

        @pl.when(slot == 1)
        def _():
            total[at(a), :] += product

    @pl.when(slot == 1)
    def _():
        begin = 0
        for out in partial:
            out[...] = total[begin : begin + out.shape[0], :].astype(BF)
            begin += out.shape[0]


def attend(y, group, qkv, halo, seg_query, seg_key, w_out):
    slots, reach, lanes = qkv.shape
    rows, width = reach // 2, w_out.shape[-1]
    sizes = (rows, rows // 2, rows // 2) if group else (rows, rows)
    return call(
        attend_kernel,
        [shaped((size, width), BF) for size in sizes]
        + [
            shaped((slots, reach, 256), BF),
            shaped((slots, 2, reach, 1), F32),
        ],
        flops=5 * 10**9,
        moved=7 * 10**6,
        grid_spec=pltpu.PrefetchScalarGridSpec(
            num_scalar_prefetch=1,
            grid=(slots,),
            in_specs=[
                pl.BlockSpec((1, reach, lanes), lambda s, y: (s, 0, 0)),
                pl.BlockSpec((reach, lanes), lambda s, y: (0, 0)),
                pl.BlockSpec((1, 2, rows, 1), lambda s, y: (group, 0, 0, 0)),
                pl.BlockSpec((1, 4, 1, rows), lambda s, y: (group, 0, 0, 0)),
                pl.BlockSpec((1,) + w_out.shape[1:], lambda s, y: (s, 0, 0)),
            ],
            out_specs=[pl.BlockSpec((size, width), lambda s, y: (0, 0)) for size in sizes]
            + [
                pl.BlockSpec((1, reach, 256), lambda s, y: (s, 0, 0)),
                pl.BlockSpec((1, 2, reach, 1), lambda s, y: (s, 0, 0, 0)),
            ],
            scratch_shapes=[pltpu.VMEM((reach, width), F32)],
        ),
    )(y, qkv, halo, seg_query, seg_key, w_out)


def load_blocks(parts, whole, sems):
    copies, at = [], 0
    for i, part in enumerate(parts):
        copies.append(
            pltpu.make_async_copy(part, whole.at[pl.ds(at, part.shape[0])], sems.at[i])
        )
        at += part.shape[0]
    for copy in copies:
        copy.start()
    return copies


def weight_copies(me, weights, gu, down, sems):
    n_z, wide = len(weights), weights[0].shape[1]
    width = down.shape[1]
    step, ff_part = width // n_z, down.shape[0] // n_z
    half = ff_part * (width - wide) // wide
    first, second = [], []
    for r, block in enumerate(weights):
        z = me ^ r
        row = pl.multiple_of(z * ff_part, ff_part)
        if gu is not None:
            first.append(
                pltpu.make_async_copy(
                    block.at[pl.ds(0, step)],
                    gu.at[pl.ds(pl.multiple_of(z * step, step), step)],
                    sems.at[0, r],
                )
            )
        second.append(
            pltpu.make_async_copy(
                block.at[pl.ds(step, ff_part)],
                down.at[pl.ds(row, ff_part), pl.ds(0, wide)],
                sems.at[1, r],
            )
        )
        for i in range(2):
            second.append(
                pltpu.make_async_copy(
                    block.at[pl.ds(step + ff_part, half), pl.ds(i * wide // 2, wide // 2)],
                    down.at[pl.ds(row + i * half, half), pl.ds(wide, width - wide)],
                    sems.at[2 + i, r],
                )
            )
    return first + second


def mlp_kernel(n_z, z_ref, *refs):
    n_parts, d_parts, refs = refs[:5], refs[5:10], refs[10:]
    w_own, w_core, refs = refs[:n_z], refs[n_z : 2 * n_z], refs[2 * n_z :]
    hidden, grad_gu, *grad_in, normed_out, upstream_out = refs[:9]
    normed, upstream, gu, down, total, n_sems, d_sems, w_sems, out_sems = refs[9:]
    slot = pl.program_id(0)
    ff = gu.shape[2] // 2
    core_copies = weight_copies(z_ref[0], w_core, gu.at[1], down.at[1], w_sems.at[1])
    kept = [
        pltpu.make_async_copy(normed, normed_out, out_sems.at[0]),
        pltpu.make_async_copy(upstream, upstream_out, out_sems.at[1]),
    ]

    @pl.when(slot == 0)
    def _():
        copies = load_blocks(n_parts, normed, n_sems)
        copies += weight_copies(z_ref[0], w_own, gu.at[0], down.at[0], w_sems.at[0])
        for copy in copies[5:]:
            copy.start()
        copies += load_blocks(d_parts, upstream, d_sems)
        for copy in core_copies:
            copy.start()
        for copy in copies:
            copy.wait()
        for copy in kept:
            copy.start()

    @pl.when(slot == 1)
    def _():
        for copy in core_copies:
            copy.wait()

    n, dy = normed[...], upstream[...]
    gate = dot(n, gu[slot, :, :ff])
    up = dot(n, gu[slot, :, ff:])
    dh = dot_nt(dy, down[slot])
    sigmoid = jax.nn.sigmoid(gate)
    silu = gate * sigmoid
    hidden[0] = (silu * up).astype(BF)
    d_gate = (dh * up * sigmoid * (1.0 + gate * (1.0 - sigmoid))).astype(BF)
    d_up = (dh * silu).astype(BF)
    grad_gu[0, :, :ff] = d_gate
    grad_gu[0, :, ff:] = d_up
    part = dot_nt(d_gate, gu[slot, :, :ff]) + dot_nt(d_up, gu[slot, :, ff:])

    @pl.when(slot == 0)
    def _():
        total[...] = part

    @pl.when(slot == 1)
    def _():
        whole = (total[...] + part).astype(BF)
        begin = 0
        for out in grad_in:
            out[...] = whole[begin : begin + out.shape[0]]
            begin += out.shape[0]
        for copy in kept:
            copy.wait()


def feed_forward(z, normed, upstream, w_own, w_core):
    rows, width = normed[0].shape
    n_z, wide = len(w_own), w_own[0].shape[1]
    tokens, ff = 4 * rows, wide // 2
    anywhere = pl.BlockSpec(memory_space=pl.ANY)
    block = pl.BlockSpec((rows, width), lambda s, z: (0, 0))
    half = pl.BlockSpec((rows // 2, width), lambda s, z: (0, 0))
    return call(
        functools.partial(mlp_kernel, n_z),
        [
            shaped((2, tokens, ff), BF),
            shaped((2, tokens, wide), BF),
            shaped((rows, width), BF),
            shaped((rows, width), BF),
            shaped((rows, width), BF),
            shaped((rows // 2, width), BF),
            shaped((rows // 2, width), BF),
            shaped((tokens, width), BF),
            shaped((tokens, width), BF),
        ],
        flops=10 * tokens * width * wide,
        moved=25 * 10**6,
        grid_spec=pltpu.PrefetchScalarGridSpec(
            num_scalar_prefetch=1,
            grid=(2,),
            in_specs=[anywhere] * (10 + 2 * n_z),
            out_specs=[
                pl.BlockSpec((1, tokens, ff), lambda s, z: (s, 0, 0)),
                pl.BlockSpec((1, tokens, wide), lambda s, z: (s, 0, 0)),
                block,
                block,
                block,
                half,
                half,
                anywhere,
                anywhere,
            ],
            scratch_shapes=[
                pltpu.VMEM((tokens, width), BF),
                pltpu.VMEM((tokens, width), BF),
                pltpu.VMEM((2, width, wide), BF),
                pltpu.VMEM((2, ff, width), BF),
                pltpu.VMEM((tokens, width), F32),
                pltpu.SemaphoreType.DMA((5,)),
                pltpu.SemaphoreType.DMA((5,)),
                pltpu.SemaphoreType.DMA((2, 4, n_z)),
                pltpu.SemaphoreType.DMA((2,)),
            ],
        ),
    )(z, *normed, *upstream, *w_own, *w_core)


def down_kernel(n_z, z_ref, hidden, *refs):
    w_own, w_core, refs = refs[:n_z], refs[n_z : 2 * n_z], refs[2 * n_z :]
    *outs, down, total, sems = refs
    slot = pl.program_id(0)
    core_copies = weight_copies(z_ref[0], w_core, None, down.at[1], sems.at[1])

    @pl.when(slot == 0)
    def _():
        copies = weight_copies(z_ref[0], w_own, None, down.at[0], sems.at[0])
        for copy in copies + core_copies:
            copy.start()
        for copy in copies:
            copy.wait()

    @pl.when(slot == 1)
    def _():
        for copy in core_copies:
            copy.wait()

    part = dot(hidden[0], down[slot])

    @pl.when(slot == 0)
    def _():
        total[...] = part

    @pl.when(slot == 1)
    def _():
        whole, begin = (total[...] + part).astype(BF), 0
        for out in outs:
            out[...] = whole[begin : begin + out.shape[0]]
            begin += out.shape[0]


def down_project(z, hidden, w_own, w_core, width):
    _, tokens, ff = hidden.shape
    n_z, rows = len(w_own), tokens // 4
    sizes = (rows, rows, rows, rows // 2, rows // 2)
    return call(
        functools.partial(down_kernel, n_z),
        [shaped((size, width), BF) for size in sizes],
        flops=4 * tokens * width * ff,
        moved=8 * 10**6,
        grid_spec=pltpu.PrefetchScalarGridSpec(
            num_scalar_prefetch=1,
            grid=(2,),
            in_specs=[pl.BlockSpec((1, tokens, ff), lambda s, z: (s, 0, 0))]
            + [pl.BlockSpec(memory_space=pl.ANY)] * (2 * n_z),
            out_specs=[pl.BlockSpec((size, width), lambda s, z: (0, 0)) for size in sizes],
            scratch_shapes=[
                pltpu.VMEM((2, ff, width), BF),
                pltpu.VMEM((tokens, width), F32),
                pltpu.SemaphoreType.DMA((2, 4, n_z)),
            ],
        ),
    )(z, hidden, *w_own, *w_core)


def grads_kernel(left, right, *rest):
    grad = dot_tn(left[...].reshape(left.shape[-2:]), right[...].reshape(right.shape[-2:]))
    if len(rest) == 2:
        grad = grad + rest[0][...].astype(F32)
    rest[-1][...] = grad.astype(BF)


def weight_grads(left, left_slot, right, right_slot, steps, *other):
    tokens, rows, columns = left.shape[-2], left.shape[-1], right.shape[-1]
    block = pl.BlockSpec((rows, columns // steps), lambda i: (0, i))

    def part(array, slot, blocks):
        if array.ndim == 2:
            return pl.BlockSpec((tokens, array.shape[1] // blocks), lambda i: (0, i if blocks > 1 else 0))
        return pl.BlockSpec(
            (1, tokens, array.shape[2] // blocks), lambda i: (slot, 0, i if blocks > 1 else 0)
        )

    return call(
        grads_kernel,
        shaped((rows, columns), BF),
        flops=2 * tokens * rows * columns,
        moved=10 * 10**6,
        grid=(steps,),
        in_specs=[part(left, left_slot, 1), part(right, right_slot, steps)] + [block] * len(other),
        out_specs=block,
    )(left, right, *other)


def cut_kernel(place_ref, w_gate, w_up, mine, other):
    ff = mine.shape[1] // 2
    for to, y in ((mine, place_ref[1]), (other, 1 - place_ref[1])):
        for i, w in enumerate((w_gate, w_up)):
            for z in range(ff // 128):
                at = pl.multiple_of(((2 * z + y) * 4 + place_ref[0]) * 128, 128)
                begin = i * ff + z * 128
                to[:, begin : begin + 128] = w[:, pl.ds(at, 128)]


def cut_columns(place, w_gate, w_up, columns):
    vmem = pl.BlockSpec(memory_space=pltpu.VMEM)
    return call(
        cut_kernel,
        [shaped((w_gate.shape[0], columns), BF)] * 2,
        flops=10**6,
        moved=8 * 10**6,
        in_specs=[pl.BlockSpec(memory_space=pltpu.SMEM)] + [vmem] * 2,
        out_specs=[vmem] * 2,
    )(place, w_gate, w_up)


def place_kernel(z_ref, own, core, out):
    rows = own.shape[1]
    for slot, pieces in enumerate((own, core)):
        for k in range(own.shape[0]):
            to = pl.multiple_of((z_ref[0] ^ k) * rows, rows)
            out[slot, pl.ds(to, rows), :] = pieces[k]


def place(z, own, core):
    n, rows, columns = own.shape
    vmem = pl.BlockSpec(memory_space=pltpu.VMEM)
    return call(
        place_kernel,
        shaped((2, n * rows, columns), BF),
        flops=10**6,
        moved=8 * n * rows * columns,
        in_specs=[pl.BlockSpec(memory_space=pltpu.SMEM)] + [vmem] * 2,
        out_specs=vmem,
    )(z, own, core)


def turn_back(values, cosine, sine):
    lane = iota(values.shape, 1)
    across = values * sine
    moved = jnp.where(
        lane < HEAD // 2,
        pltpu.roll(across, 128 - HEAD // 2, 1),
        jnp.where(lane < HEAD, -pltpu.roll(across, HEAD // 2, 1), 0.0),
    )
    return values * cosine + moved


def attend_back_kernel(n_parts, *refs):
    y_ref, qkv, halo, seg_query, seg_key, w_out, context, logsum, cosine, sine = refs[:10]
    parts, rest = refs[10 : 10 + n_parts], refs[10 + n_parts :]
    before = rest[0] if len(rest) == 9 else None
    grad_query, grad_kv, grad_halo, grad_out, up, kv_total, out_total, sems = rest[-8:]
    slot = pl.program_id(0)
    reach = qkv.shape[1]
    rows = reach // 2
    factor = 1.0 / math.sqrt(HEAD)

    @pl.when(slot == 0)
    def _():
        for copy in load_blocks(parts, up, sems):
            copy.wait()

    at, query, key_value = heads_of(y_ref[0], slot, qkv, halo, rows)
    w = padded_out(w_out)
    kv_total[...] = jnp.zeros_like(kv_total)
    out_part = None
    for a in range(2):
        dy = up[at(a), :]
        d_context = dot_nt(dy, w).astype(BF)
        part = dot_tn(context[0, at(a), :], dy)
        out_part = part if out_part is None else out_part + part
        d_seen = jnp.concatenate([d_context[:, :128], d_context[:, 128:]], axis=0)
        kv = jnp.concatenate(key_value[a : a + 3], axis=0)
        key, value = kv[:, :128], kv[:, 128:]
        scores = dot_nt(query[a], key) * factor
        probs = jnp.exp(
            jnp.where(visible(seg_query, seg_key, a, rows), scores - logsum[0, a], -1e30)
        )
        d_probs = dot_nt(d_seen, value)
        delta = jnp.sum(probs * d_probs, axis=-1, keepdims=True)
        d_scores = (probs * (d_probs - delta)).astype(BF)
        d_query = dot(d_scores, key) * factor
        cos_a, sin_a = cosine[at(a), :], sine[at(a), :]
        turned = jnp.concatenate(
            [turn_back(d_query[:rows], cos_a, sin_a), turn_back(d_query[rows:], cos_a, sin_a)],
            axis=1,
        ).astype(BF)
        grad_query[0, at(a), :] = dot(turned, pack(qkv.shape[-1], 2, 0)).astype(BF)
        seen = slice(a * rows, (a + 3) * rows)
        kv_total[seen, :128] += dot_tn(d_scores, query[a]) * factor
        kv_total[seen, 128:] += dot_tn(probs.astype(BF), d_seen)
    back = pack(qkv.shape[-1], 2, (1 - slot) * (qkv.shape[-1] // 2))
    for a in range(2):
        grad_kv[0, at(a), :] = kv_total[(a + 2) * rows : (a + 3) * rows, :]
        placed = dot(kv_total[a * rows : (a + 1) * rows, :].astype(BF), back).astype(BF)

        @pl.when(slot == 0)
        def _():
            grad_halo[at(a), :] = placed

        @pl.when(slot == 1)
        def _():
            grad_halo[at(a), :] += placed

    out_total[...] = out_part.astype(BF)
    part = dot(spread(w_out.shape[1], 2, 0), out_total[...])
    if before is not None:
        part = part + before[0].astype(F32)
    grad_out[0] = part.astype(BF)


def attend_back(y, group, qkv, halo, seg_query, seg_key, w_out, context, logsum, cosine, sine, upstream, before=()):
    slots, reach, lanes = qkv.shape
    rows, width = reach // 2, w_out.shape[-1]
    weight = pl.BlockSpec((1,) + w_out.shape[1:], lambda s, y: (s, 0, 0))
    return call(
        functools.partial(attend_back_kernel, len(upstream)),
        [
            shaped((slots, reach, lanes), BF),
            shaped((slots, reach, 256), F32),
            shaped((reach, lanes), BF),
            shaped(w_out.shape, BF),
        ],
        flops=12 * 10**9,
        moved=10 * 10**6,
        grid_spec=pltpu.PrefetchScalarGridSpec(
            num_scalar_prefetch=1,
            grid=(slots,),
            in_specs=[
                pl.BlockSpec((1, reach, lanes), lambda s, y: (s, 0, 0)),
                pl.BlockSpec((reach, lanes), lambda s, y: (0, 0)),
                pl.BlockSpec((1, 2, rows, 1), lambda s, y: (group, 0, 0, 0)),
                pl.BlockSpec((1, 4, 1, rows), lambda s, y: (group, 0, 0, 0)),
                weight,
                pl.BlockSpec((1, reach, 256), lambda s, y: (s, 0, 0)),
                pl.BlockSpec((1, 2, reach, 1), lambda s, y: (s, 0, 0, 0)),
                pl.BlockSpec((reach, 128), lambda s, y: (group, 0)),
                pl.BlockSpec((reach, 128), lambda s, y: (group, 0)),
            ]
            + [pl.BlockSpec(memory_space=pl.ANY)] * len(upstream)
            + [weight] * len(before),
            out_specs=[
                pl.BlockSpec((1, reach, lanes), lambda s, y: (s, 0, 0)),
                pl.BlockSpec((1, reach, 256), lambda s, y: (s, 0, 0)),
                pl.BlockSpec((reach, lanes), lambda s, y: (0, 0)),
                weight,
            ],
            scratch_shapes=[
                pltpu.VMEM((reach, width), BF),
                pltpu.VMEM((2 * reach, 256), F32),
                pltpu.VMEM((256, width), BF),
                pltpu.SemaphoreType.DMA((len(upstream),)),
            ],
        ),
    )(y, qkv, halo, seg_query, seg_key, w_out, context, logsum, cosine, sine, *upstream, *before)


def qkv_back_kernel(grad_query, grad_kv, grad_halo, cosine, sine, w_own, w_core, grad_qkv, *grad_in):
    lanes = grad_halo.shape[-1]
    total = None
    place = pack(lanes, 2, lanes // 2)
    size = grad_in[0].shape[1] // w_own.shape[0]
    for slot, w in enumerate((w_own, w_core)):
        kv = grad_kv[slot] + dot(grad_halo[...], spread(lanes, 2, (1 - slot) * (lanes // 2)))
        key = turn_back(kv[:, :128], cosine[...], sine[...])
        kv = jnp.concatenate([key, kv[:, 128:]], axis=1).astype(BF)
        both = grad_query[slot] + dot(kv, place).astype(BF)
        grad_qkv[slot] = both
        part = [dot_nt(both, w[z, :size, :]) for z in range(w.shape[0])]
        part = jnp.concatenate(part, axis=1)
        total = part if total is None else total + part
    whole, begin = total.astype(BF), 0
    for out in grad_in:
        out[...] = whole[begin : begin + out.shape[0]]
        begin += out.shape[0]


def qkv_back(group, grad_query, grad_kv, grad_halo, cosine, sine, w_own, w_core, width):
    slots, tokens, lanes = grad_query.shape
    rows = tokens // 2
    sizes = (rows, rows // 2, rows // 2) if group else (rows, rows)
    table = pl.BlockSpec((tokens, 128), lambda i: (group, 0))

    def whole(array):
        return pl.BlockSpec(array.shape, lambda i: (0,) * array.ndim)

    outs = [shaped((slots, tokens, lanes), BF)] + [shaped((size, width), BF) for size in sizes]
    return call(
        qkv_back_kernel,
        outs,
        flops=2 * slots * tokens * width * lanes,
        moved=6 * 10**6,
        grid=(1,),
        in_specs=[whole(grad_query), whole(grad_kv), whole(grad_halo), table, table]
        + [whole(w_own), whole(w_core)],
        out_specs=[whole(out) for out in outs],
    )(grad_query, grad_kv, grad_halo, cosine, sine, w_own, w_core)


def lay_out_kernel(d_ref, *refs):
    b0, b1, b2, b3, w_gate, w_up, gain, out_gate, out_up, grad_gain = refs
    ff = b0.shape[2] // 2
    for k, block in enumerate((b0, b1, b2, b3)):
        for y in range(2):
            for z in range(ff // 128):
                to = pl.multiple_of(((2 * z + y) * 4 + (d_ref[0] ^ k)) * 128, 128)
                out_gate[:, pl.ds(to, 128)] = block[y, :, z * 128 : (z + 1) * 128].astype(F32)
                out_up[:, pl.ds(to, 128)] = block[y, :, ff + z * 128 : ff + (z + 1) * 128].astype(F32)
    weighted = w_gate[...].astype(F32) * out_gate[...] + w_up[...].astype(F32) * out_up[...]
    grad_gain[...] = jnp.sum(weighted, axis=-1, keepdims=True) / gain[...]


def lay_out(d, blocks, w_gate, w_up, gain):
    shard, ff = w_gate.shape
    rows = 64
    blocks = [block.reshape(2, shard, block.shape[1]) for block in blocks]
    part = pl.BlockSpec((2, rows, blocks[0].shape[2]), lambda i, d: (0, i, 0))
    whole = pl.BlockSpec((rows, ff), lambda i, d: (i, 0))
    column = pl.BlockSpec((rows, 1), lambda i, d: (i, 0))
    return call(
        lay_out_kernel,
        [shaped((shard, ff), F32), shaped((shard, ff), F32), shaped((shard, 1), F32)],
        flops=6 * shard * ff,
        moved=16 * shard * ff,
        grid_spec=pltpu.PrefetchScalarGridSpec(
            num_scalar_prefetch=1,
            grid=(shard // rows,),
            in_specs=[part] * 4 + [whole, whole, column],
            out_specs=[whole, whole, column],
        ),
    )(d, *blocks, w_gate, w_up, gain)


def lay_out_rows_kernel(d_ref, b0, b1, b2, b3, out):
    rows = b0.shape[0]
    for k, block in enumerate((b0, b1, b2, b3)):
        at = pl.ds(pl.multiple_of((d_ref[0] ^ k) * rows, rows), rows)
        out[at, :] = block[...].astype(F32)


def lay_out_rows(d, blocks):
    rows, width = blocks[0].shape
    vmem = pl.BlockSpec(memory_space=pltpu.VMEM)
    return call(
        lay_out_rows_kernel,
        shaped((4 * rows, width), F32),
        flops=rows * width,
        moved=24 * rows * width,
        in_specs=[pl.BlockSpec(memory_space=pltpu.SMEM)] + [vmem] * 4,
        out_specs=vmem,
    )(d, *blocks)


def lay_out_heads_kernel(d_ref, *refs):
    blocks, (w_query, w_key, w_value, gain) = refs[:4], refs[4:8]
    out_query, out_key, out_value, out_out, grad_gain, ordered = refs[8:]
    shard, lanes = w_query.shape[0], blocks[0].shape[1]
    count = out_out.shape[0] // 4
    for k, block in enumerate(blocks):
        to = d_ref[0] ^ k
        ordered[to] = block[: 2 * shard, :]
        at = pl.ds(pl.multiple_of(to * count, count), count)
        for i in range(4):
            out_out[at, i * lanes : (i + 1) * lanes] = block[
                2 * shard + i * count : 2 * shard + (i + 1) * count, :
            ].astype(F32)
    row, column = iota((lanes, lanes), 0), iota((lanes, lanes), 1)

    def place(begin, count, to):
        hit = (column - to == row - begin) & (row >= begin) & (row < begin + count)
        return jnp.where(hit, 1.0, 0.0).astype(BF)

    def block_of(t):
        return ordered[t // 2, (t % 2) * shard : (t % 2 + 1) * shard, :]

    total = None
    for begin, count, out, w in (
        (0, 2 * HEAD, out_query, w_query),
        (2 * HEAD, HEAD, out_key, w_key),
        (3 * HEAD, HEAD, out_value, w_value),
    ):
        heads = lanes // count
        places = [place(begin, count, i * count) for i in range(heads)]
        for j in range(KV_HEADS // heads):
            piece = None
            for i in range(heads):
                part = dot(block_of(j * heads + i), places[i])
                piece = part if piece is None else piece + part
            at = slice(j * lanes, (j + 1) * lanes)
            out[:, at] = piece
            part = jnp.sum(w[:, at].astype(F32) * piece, axis=-1, keepdims=True)
            total = part if total is None else total + part
    grad_gain[...] = total / gain[...]


def lay_out_heads(d, blocks, w_query, w_key, w_value, gain, out_shape):
    shard = w_query.shape[0]
    vmem = pl.BlockSpec(memory_space=pltpu.VMEM)
    return call(
        lay_out_heads_kernel,
        [
            shaped(w_query.shape, F32),
            shaped(w_key.shape, F32),
            shaped(w_value.shape, F32),
            shaped(out_shape, F32),
            shaped((shard, 1), F32),
        ],
        flops=4 * 10**9,
        moved=8 * 10**6,
        in_specs=[pl.BlockSpec(memory_space=pltpu.SMEM)] + [vmem] * 8,
        out_specs=[vmem] * 5,
        scratch_shapes=[pltpu.VMEM((4, 2 * shard, blocks[0].shape[1]), BF)],
    )(d, *blocks, w_query, w_key, w_value, gain)


def layout_rows(lengths, index):
    ends = jnp.cumsum(lengths, axis=1)
    before = index[None, :, None] >= ends[:, None, :]
    segment = jnp.sum(before.astype(jnp.int32), axis=2)
    offset = jnp.sum(jnp.where(before, lengths[:, None, :], 0), axis=2)
    segment = jnp.where(segment < lengths.shape[1], segment, -1)
    segment = jnp.where(index[None, :] < 0, -3, segment)
    return (segment, index[None, :] - offset)


def on_device(
    tokens,
    lengths,
    cotangent,
    gain_attn,
    w_query,
    w_key,
    w_value,
    w_out,
    gain_mlp,
    w_gate,
    w_up,
    w_down,
):
    n_dp, n_seq = lax.axis_size("dp"), lax.axis_size("seq")
    d, me = lax.axis_index("dp"), lax.axis_index("seq")
    y, n_z = me % 2, n_seq // 2
    rows, width = tokens.shape
    reach = 2 * rows
    assert WINDOW <= reach and KV_HEADS == 2 * n_dp
    groups = HEADS // KV_HEADS
    q_w, k_w = groups * HEAD, HEAD
    shard = w_query.shape[0]
    ff_shard = w_down.shape[0]
    ff_part = ff_shard // n_dp

    def head_columns(j):
        t = 2 * d + j
        gains = jnp.zeros((16, q_w + 2 * k_w), BF)
        gains = gains.at[0, :shard].set(gain_attn).at[1, :shard].set(gain_mlp)
        columns = jnp.concatenate(
            [
                lax.dynamic_slice_in_dim(w_query, t * q_w, q_w, 1),
                lax.dynamic_slice_in_dim(w_key, t * k_w, k_w, 1),
                lax.dynamic_slice_in_dim(w_value, t * k_w, k_w, 1),
            ],
            axis=1,
        )
        return jnp.concatenate([columns, gains], axis=0)

    def ff_columns(j):
        parts = [
            lax.dynamic_slice_in_dim(w, ((2 * z + j) * n_dp + d) * ff_part, ff_part, 1)
            for w in (gate_in, up_in)
            for z in range(n_z)
        ]
        return jnp.concatenate(parts, axis=1)

    lanes = q_w + 2 * k_w
    square = n_seq == 2 * n_dp
    d_arg = jnp.reshape(d, (1,)).astype(jnp.int32)
    z_arg = jnp.reshape(me // 2, (1,)).astype(jnp.int32)

    lens_far = send(lengths, across_x)
    qkv_from_y = send(head_columns(1 - y), across_y)
    tokens_all = gather_plane(tokens, for_y=after(tokens, qkv_from_y))
    low, high = pair_y(head_columns(y), qkv_from_y)
    gain_rows = jnp.concatenate([low[shard:, :shard], high[shard:, :shard]], axis=1)
    gain_rows = jnp.pad(gain_rows, ((0, 0), (0, lanes - 2 * shard)))
    part_qkv = jnp.concatenate([low[:shard], high[:shard], gain_rows], axis=0)
    own_qkv = gather_z(part_qkv)
    lens = jnp.concatenate([lengths, after(lens_far, tokens_all[3])], axis=0)

    first_row = (me // 2) * reach
    steps = jnp.arange(reach, dtype=jnp.int32)
    order = jnp.arange(2, dtype=jnp.int32)[:, None] ^ y
    _, position = layout_rows(lens, first_row + (order * rows + steps[None, :rows]).reshape(-1))
    cosine, sine = rope_tables(position.reshape(-1))
    key_index = first_row - reach + jnp.arange(2 * reach, dtype=jnp.int32)
    segment, _ = layout_rows(lens, key_index)
    segment = jnp.where(segment == -1, -8 - key_index[None, :], segment)
    seg_key = segment.reshape(2, 4, 1, rows)
    seg_query = segment[:, reach:].reshape(2, 2, rows, 1)
    y_arg = jnp.reshape(y, (1,)).astype(jnp.int32)

    gate_in, up_in = lax.optimization_barrier((w_gate, w_up, qkv_from_y))[:2]
    if ff_part % 128 == 0:
        here = jnp.stack([d, y]).astype(jnp.int32)
        mine_ff, other_ff = cut_columns(here, gate_in, up_in, 2 * n_z * ff_part)
    else:
        mine_ff, other_ff = ff_columns(y), ff_columns(1 - y)
    other_ff = send(after(other_ff, tokens_all[1]), across_y)
    part_mlp = jnp.concatenate(
        [
            pair_y(mine_ff, other_ff).reshape(2 * shard, -1),
            fold(lax.dynamic_slice_in_dim(w_down, d * ff_part, ff_part, 0), 2 * n_z * ff_part),
        ],
        axis=0,
    )
    early = ()
    if square:
        out_rows = shard // n_dp
        part_out = lax.dynamic_slice_in_dim(w_out, d * out_rows, out_rows, 0)
        part_out = send(after(part_out, part_qkv), turned)
        early = (part_out,)
    own_qkv = lax.optimization_barrier((own_qkv, part_mlp, cosine, *early, *tokens_all))[0]
    core_qkv = send(own_qkv, across_core)
    if square:
        out_pieces = [send(after(part_out, own_qkv), across_z(k)) for k in (1, 2, 3)]
    else:
        own_out = lax.all_gather(w_out, "seq", axis=0, tiled=True)
        own_out = lax.dynamic_slice_in_dim(own_out, (2 * d + y) * q_w, q_w, 0)
    full_qkv = [own_qkv, core_qkv]
    if not square:
        full_qkv = [part[:, : 2 * shard].reshape(1, width, lanes) for part in full_qkv]
    gains = own_qkv[:, 2 * shard : 2 * shard + 2, : 2 * shard]
    full_gain_attn = gains[:, 0].reshape(1, -1).astype(F32)
    full_gain_mlp = gains[:, 1].reshape(1, -1).astype(F32)

    groups_of = ((0, 1), (2, 3, 4))

    def parts_of(pieces, group):
        return [pieces[i] for i in groups_of[group]]

    normed, qkv, halo, halo_in = [None] * 2, [None] * 2, [None] * 2, [None] * 2
    for group in (1, 0):
        normed[group], qkv[group], halo[group] = project(
            group, parts_of(tokens_all, group), full_gain_attn, cosine, sine, *full_qkv
        )
        halo_in[group] = send(halo[group], lambda d, s: (d, s + 2))
    if square:
        out_pieces = lax.optimization_barrier((*out_pieces, *halo))[:3]
        own_out = jnp.stack([part_out, *out_pieces])
        full_out = place(z_arg, own_out, send(own_out, across_core))
    else:
        full_out = jnp.stack(with_core(own_out))
    part_ready = lax.optimization_barrier((part_mlp, *halo_in))[0]
    if square:
        both = send(part_ready, across_z(2))
        mlp_near = send(part_ready, across_z(1))
    else:
        blocks = gather_z(part_ready)
        down_rows = jnp.concatenate([unfold(blocks[z, 2 * shard :], width) for z in range(n_z)], axis=0)
        own_mlp = [
            jnp.concatenate(
                [blocks[:, : 2 * shard].reshape(width, -1), fold(down_rows, 2 * n_z * ff_part)], axis=0
            )
        ]
    cotangent_in = after(cotangent, *tokens_all)
    came = (send(cotangent_in, across_x), send(cotangent_in, across_y))
    upstream_all = gather_plane(cotangent, *halo, came=came)
    halo_first = lax.optimization_barrier((halo_in[0], *upstream_all))[0]
    partial, context, logsum = [None] * 2, [None] * 2, [None] * 2
    for group in (1, 0):
        *partial[group], context[group], logsum[group] = attend(
            y_arg, group, qkv[group], halo_in[1] if group else halo_first, seg_query, seg_key, full_out
        )
    arrived = (both, mlp_near) if square else ()
    middle = tokens.astype(F32) + scatter_plane(*partial, *arrived)


    inverse_mlp = lax.rsqrt(jnp.mean(middle * middle, axis=-1, keepdims=True) + EPS)
    normed_mlp_own = (middle * inverse_mlp * full_gain_mlp).astype(BF)
    if square:
        mlp_far = both
        own_mlp = [part_mlp, mlp_near, mlp_far, send(mlp_far, across_z(1))]
    normed_mlp_all = gather_plane(normed_mlp_own)
    core_mlp = [send(block, across_core) for block in own_mlp]
    z_own = z_arg if square else jnp.zeros_like(z_arg)
    hidden, grad_gu, *grad_in, normed_mlp, upstream_low = feed_forward(
        z_own, normed_mlp_all, upstream_all, own_mlp, core_mlp
    )
    grad_near, grad_far = grad_in[:2], grad_in[2:]
    from_core_gu = send(weight_grads(normed_mlp, 0, grad_gu, 1, 2), across_core)
    down_core = weight_grads(hidden, 1, upstream_low, 0, 1)
    grad_w_gu = weight_grads(normed_mlp, 0, grad_gu, 0, 2, from_core_gu)
    grad_normed_mlp = scatter_plane(grad_near, grad_far, at_first=(down_core, grad_w_gu))
    got_gu = along_z(grad_w_gu.reshape(n_z, 2 * shard, -1))
    total_gu = jnp.sum(got_gu.astype(F32), axis=0).astype(BF)
    upstream = cotangent.astype(F32)
    scaled = grad_normed_mlp * full_gain_mlp
    grad_middle = (
        upstream
        + inverse_mlp * scaled
        - middle * inverse_mlp**3 * jnp.mean(scaled * middle, axis=-1, keepdims=True)
    )
    down = down_project(z_own, hidden, own_mlp, core_mlp, width)
    from_core = send(down_core, across_core)
    grad_w_down = weight_grads(hidden, 0, upstream_low, 0, 1, from_core)
    grad_attended_all = gather_plane(
        after(grad_middle.astype(BF), grad_w_gu), *down, grad_w_down
    )
    down = lax.optimization_barrier((*down, *grad_attended_all))[:5]
    (own, own_y), (far, far_a, far_b) = down[:2], down[2:]
    half = rows // 2
    first, second = send(far_a, across_y), send(far_b, across_x)

    def swap_rows(total):
        mine = lax.dynamic_slice_in_dim(total, y * shard, shard, 0)
        other = lax.dynamic_slice_in_dim(total, (1 - y) * shard, shard, 0)
        return pair_y(mine, send(other, across_y)).reshape(2 * shard, -1)

    mine_gu = swap_rows(total_gu)
    gu_blocks = gather_dp(mine_gu)
    if ff_part % 128 == 0:
        gain_column = gain_mlp.astype(F32).reshape(-1, 1)
        out_gate, out_up, grad_gain_mlp = lay_out(d_arg, gu_blocks, w_gate, w_up, gain_column)
    else:
        all_gu = jnp.stack(order_dp(gu_blocks)).reshape(n_dp, 2, shard, 2, n_z, ff_part)
        all_gu = all_gu.transpose(3, 2, 4, 1, 0, 5).reshape(2, shard, -1).astype(F32)
        out_gate, out_up = all_gu[0], all_gu[1]
        grad_gain_mlp = jnp.sum(
            w_gate.astype(F32) * out_gate + w_up.astype(F32) * out_up, axis=1
        ) / gain_mlp.astype(F32)

    grad_query, grad_kv, halo_back = [None] * 2, [None] * 2, [None] * 2
    grad_out = ()
    for group in (0, 1):
        dy = parts_of(grad_attended_all, group)
        grad_query[group], grad_kv[group], grad_halo, grad_out = attend_back(
            y_arg, group, qkv[group], halo_in[group], seg_query, seg_key, full_out,
            context[group], logsum[group], cosine, sine, dy, (grad_out,) if group else (),
        )
        grad_halo, first, second = lax.optimization_barrier((grad_halo, first, second, got_gu))[:3]
        halo_back[group] = send(grad_halo, lambda d, s: (d, s - 2))
    grad_qkv, grad_in = [None] * 2, [None] * 2
    far = jnp.concatenate([plus(far[:half], first), far[half:]], axis=0)
    own_y = jnp.concatenate([own_y[:half], plus(own_y[half:], second)], axis=0)
    down_x, down_y = send(far, across_x), send(own_y, across_y)
    halo_back[1] = after(halo_back[1], mine_gu)
    for group in (0, 1):
        grad_qkv[group], *grad_in[group] = qkv_back(
            group, grad_query[group], grad_kv[group], halo_back[group], cosine, sine, *full_qkv, width
        )
    grad_w_down = lax.optimization_barrier((grad_w_down, halo_back[1]))[0]
    total_down = scatter_z(grad_w_down.reshape(n_z, ff_part, width)).astype(BF)
    out_down = lay_out_rows(d_arg, gather_dp(total_down))

    def attn_grads(slot):
        for_qkv = dot_tn(normed[0], grad_qkv[0][slot]) + dot_tn(normed[1], grad_qkv[1][slot])
        for_qkv = for_qkv.astype(BF).reshape(n_z, 2 * shard, -1)
        if not square:
            return for_qkv
        for_out = [
            fold(grad_out[slot, z * out_rows : (z + 1) * out_rows], lanes) for z in range(n_z)
        ]
        return jnp.concatenate([for_qkv, jnp.stack(for_out)], axis=1)

    grad_attn = sum_core(attn_grads(0), attn_grads(1))
    output = (
        middle + own.astype(F32) + down_x.astype(F32) + down_y.astype(F32)
    ).astype(BF)
    total_attn = along_z(grad_attn)
    total_attn = jnp.sum(total_attn.astype(F32), axis=0).astype(BF)
    mine_attn = swap_rows(total_attn[: 2 * shard]).reshape(2 * shard, -1)
    if square:
        mine_attn = jnp.concatenate([mine_attn, send(total_attn[2 * shard :], turned)], axis=0)
    attn_blocks = gather_dp(mine_attn, out_gate, out_down)
    if square:
        out_query, out_key, out_value, out_out, grad_gain_attn = lay_out_heads(
            d_arg, attn_blocks, w_query, w_key, w_value, gain_attn.astype(F32).reshape(-1, 1), w_out.shape
        )
    else:
        attn_blocks = order_dp(attn_blocks)
        grad_w_out = sum_core(grad_out[0], grad_out[1]).astype(F32)
        out_out = jnp.zeros((2 * n_dp * q_w, width), F32)
        out_out = lax.dynamic_update_slice_in_dim(out_out, grad_w_out, (2 * d + y) * q_w, 0)
        out_out = lax.psum_scatter(out_out, "seq", scatter_dimension=0, tiled=True)
        out_out = lax.psum(out_out.astype(BF), "dp").astype(F32)
        all_qkv = jnp.stack(attn_blocks).astype(F32)
        out_qkv = all_qkv.reshape(2 * n_dp, shard, lanes).transpose(1, 0, 2)
        out_query = out_qkv[..., :q_w].reshape(shard, -1)
        out_key = out_qkv[..., q_w : q_w + k_w].reshape(shard, -1)
        out_value = out_qkv[..., q_w + k_w :].reshape(shard, -1)
        grad_gain_attn = (
            jnp.sum(w_query.astype(F32) * out_query, axis=1)
            + jnp.sum(w_key.astype(F32) * out_key, axis=1)
            + jnp.sum(w_value.astype(F32) * out_value, axis=1)
        ) / gain_attn.astype(F32)

    own = scatter_plane(*grad_in, at_first=(down_x, down_y))
    wide = tokens.astype(F32)
    own_inverse = lax.rsqrt(jnp.mean(wide * wide, axis=-1, keepdims=True) + EPS)
    scaled = own * full_gain_attn
    grad_tokens = (
        grad_middle
        + own_inverse * scaled
        - wide * own_inverse**3 * jnp.mean(scaled * wide, axis=-1, keepdims=True)
    )
    return (
        output,
        grad_tokens,
        grad_gain_attn.reshape(-1),
        out_query,
        out_key,
        out_value,
        out_out,
        grad_gain_mlp.reshape(-1),
        out_gate,
        out_up,
        out_down,
    )


def solution(mesh):
    return jax.shard_map(
        on_device,
        mesh=mesh,
        in_specs=(
            P(("dp", "seq"), None),
            P("dp", None),
            P(("dp", "seq"), None),
            P("seq"),
            P("seq", None),
            P("seq", None),
            P("seq", None),
            P("seq", None),
            P("seq"),
            P("seq", None),
            P("seq", None),
            P("seq", None),
        ),
        out_specs=(
            P(("dp", "seq"), None),
            P(("dp", "seq"), None),
            P("seq"),
            P("seq", None),
            P("seq", None),
            P("seq", None),
            P("seq", None),
            P("seq"),
            P("seq", None),
            P("seq", None),
            P("seq", None),
        ),
        check_vma=False,
    )
```

profile of v0, /device:TPU:0, one launch (start us, length us, event | category | flops | bytes accessed | tf_op | source)
XLA Modules:
  0.0 499.6 jit_solution(13634370970779593006)
XLA Ops:
  0.7 3.0 collective-permute-start.3
  9.8 3.4 collective-permute-done
  16.3 4.9 all-to-all-start
  22.7 5.6 %collective-permute-done.4.refs_0_ = bf16[256,1536]{1,0:T(8,128)(2,1)} collective-permute-done((bf16[256,1536]{1,0:T(8,128)(2,1)}, bf16[256,1536]{1,0:T(8,128)(2,1)}, u32[]{:S(2)}, u32[]{:S(2)}) %collective-permute-start.4) | collective-permute-done | bytes 786464 | tf_op jit(solution)/shard_map/ppermute | solution.py:32
  32.1 2.9 collective-permute-start.6
  35.1 3.0 shard_map.203
  39.1 3.2 collective-permute-start.7
  44.2 3.1 multiply_sine_fusion
  47.2 7.2 %collective-permute-done.2 = bf16[192,1024]{1,0:T(8,128)(2,1)S(1)} collective-permute-done((bf16[192,1024]{1,0:T(8,128)(2,1)}, bf16[192,1024]{1,0:T(8,128)(2,1)S(1)}, u32[]{:S(2)}, u32[]{:S(2)}) %collective-permute-start.2) | collective-permute-done | bytes 393248 | tf_op jit(solution)/shard_map/ppermute | solution.py:32
  60.0 4.2 collective-permute-start.14
  64.8 6.5 %shard_map.205 = (bf16[512,1536]{1,0:T(8,128)(2,1)}, bf16[2,512,384]{2,1,0:T(8,128)(2,1)}, bf16[512,384]{1,0:T(8,128)(2,1)}) custom-call(bf16[256,1536]{1,0:T(8,128)(2,1)} %collective-permute-done.4.refs_0_, bf16[128,1536]{1,0:T(8,128)(2,1)} %collective-permute-done.5.refs_1_, bf16[128,1536]{1,0:T(8,128)(2,1)} %copy-done.47, f32[1,1536]{1,0:T(1,128)} %bitcast.96, ...), custom_call_target="tpu_custom_call" | custom-call | flops 362387872 | bytes 1800000 | tf_op jit(solution)/shard_map/pallas_call | solution.py:269
  71.4 6.6 %shard_map.204 = (bf16[512,1536]{1,0:T(8,128)(2,1)}, bf16[2,512,384]{2,1,0:T(8,128)(2,1)}, bf16[512,384]{1,0:T(8,128)(2,1)}) custom-call(bf16[256,1536]{1,0:T(8,128)(2,1)} %refs_0_.1, bf16[256,1536]{1,0:T(8,128)(2,1)} %collective-permute-done.1.refs_1_, f32[1,1536]{1,0:T(1,128)} %bitcast.97, f32[1024,128]{1,0:T(8,128)} %get-tuple-element.302.refs_3_.refs_4_.refs_8_.cosine, ...), custom_call_target="tpu_custom_call" | custom-call | flops 362387872 | bytes 1800000 | tf_op jit(solution)/shard_map/pallas_call | solution.py:269
  82.2 3.0 collective-permute-start.9
  93.8 11.4 %shard_map.208 = (bf16[256,1536]{1,0:T(8,128)(2,1)}, bf16[128,1536]{1,0:T(8,128)(2,1)}, bf16[128,1536]{1,0:T(8,128)(2,1)}, bf16[2,512,256]{2,1,0:T(8,128)(2,1)}, f32[2,2,512,1]{3,2,1,0:T(8,128)}) custom-call(s32[1]{0:T(128)} %bitcast.y_ref.refs_0_, bf16[2,512,384]{2,1,0:T(8,128)(2,1)} %get-tuple-element.165.qkv.refs_1_, bf16[512,384]{1,0:T(8,128)(2,1)} %copy-done.58, ...), custom_call_target="tpu_custom_call" | custom-call | flops 1500000000 | bytes 2100000 | tf_op jit(solution)/shard_map/pallas_call | solution.py:348
  109.0 11.3 %shard_map.207 = (bf16[256,1536]{1,0:T(8,128)(2,1)}, bf16[256,1536]{1,0:T(8,128)(2,1)}, bf16[2,512,256]{2,1,0:T(8,128)(2,1)}, f32[2,2,512,1]{3,2,1,0:T(8,128)}) custom-call(s32[1]{0:T(128)} %bitcast.y_ref.refs_0_, bf16[2,512,384]{2,1,0:T(8,128)(2,1)} %get-tuple-element.153.qkv.refs_1_, bf16[512,384]{1,0:T(8,128)(2,1)} %collective-permute-done.9.halo.refs_2_, ...), custom_call_target="tpu_custom_call" | custom-call | flops 1500000000 | bytes 2100000 | tf_op jit(solution)/shard_map/pallas_call | solution.py:348
  128.3 32.0 %collective-permute-done.23.refs_12_.refs_2_ = bf16[576,1024]{1,0:T(8,128)(2,1)} collective-permute-done((bf16[576,1024]{1,0:T(8,128)(2,1)S(1)}, bf16[576,1024]{1,0:T(8,128)(2,1)}, u32[]{:S(2)}, u32[]{:S(2)}) %collective-permute-start.23) | collective-permute-done | bytes 1179680 | tf_op jit(solution)/shard_map/ppermute | solution.py:32
  166.8 15.6 %collective-permute-done.26.refs_2_ = bf16[256,1536]{1,0:T(8,128)(2,1)S(1)} collective-permute-done((bf16[256,1536]{1,0:T(8,128)(2,1)S(1)}, bf16[256,1536]{1,0:T(8,128)(2,1)S(1)}, u32[]{:S(2)}, u32[]{:S(2)}) %collective-permute-start.26) | collective-permute-done | bytes 786464 | tf_op jit(solution)/shard_map/ppermute | solution.py:32
  182.3 4.3 collective-permute-done.29.refs_13_.refs_3_
  188.0 10.2 %collective-permute-done.27.refs_3_ = bf16[128,1536]{1,0:T(8,128)(2,1)S(1)} collective-permute-done((bf16[128,1536]{1,0:T(8,128)(2,1)S(1)}, bf16[128,1536]{1,0:T(8,128)(2,1)S(1)}, u32[]{:S(2)}, u32[]{:S(2)}) %collective-permute-start.27) | collective-permute-done | bytes 393248 | tf_op jit(solution)/shard_map/ppermute | solution.py:32
  199.2 27.1 %shard_map.209 = (bf16[2,1024,512]{2,1,0:T(8,128)(2,1)}, bf16[2,1024,1024]{2,1,0:T(8,128)(2,1)}, bf16[256,1536]{1,0:T(8,128)(2,1)}, bf16[256,1536]{1,0:T(8,128)(...) custom-call(s32[1]{0:T(128)} %bitcast.6.z_ref, ...), custom_call_target="tpu_custom_call" | custom-call | flops 4831838208 | bytes 7500000 | tf_op jit(solution)/shard_map/pallas_call | solution.py:491
  226.4 7.1 %shard_map.212 = bf16[1536,1024]{1,0:T(8,128)(2,1)} custom-call(bf16[1024,1536]{1,0:T(8,128)(2,1)} %get-tuple-element.184.left, bf16[2,1024,1024]{2,1,0:T(8,128)(2,1)} %get-tuple-element.185.right), custom_call_target="tpu_custom_call" | custom-call | flops 966367616 | bytes 3000000 | tf_op jit(solution)/shard_map/pallas_call | solution.py:611
  237.4 5.2 %shard_map.211 = bf16[512,1536]{1,0:T(8,128)(2,1)} custom-call(bf16[2,1024,512]{2,1,0:T(8,128)(2,1)} %get-tuple-element.173.hidden.left, bf16[1024,1536]{1,0:T(8,128)(2,1)} %get-tuple-element.183.right), custom_call_target="tpu_custom_call" | custom-call | flops 483183808 | bytes 3000000 | tf_op jit(solution)/shard_map/pallas_call | solution.py:611
  242.6 7.9 %shard_map.213 = bf16[1536,1024]{1,0:T(8,128)(2,1)} custom-call(bf16[1024,1536]{1,0:T(8,128)(2,1)} %get-tuple-element.184.left, bf16[2,1024,1024]{2,1,0:T(8,128)(2,1)} %get-tuple-element.185.right, bf16[1536,1024]{1,0:T(8,128)(2,1)} %collective-permute-done.36.rest_0_), custom_call_target="tpu_custom_call" | custom-call | flops 966367616 | bytes 3000000 | tf_op jit(solution)/shard_map/pallas_call | solution.py:611
  254.8 4.8 all-to-all-start.1
  259.6 12.7 %collective-permute-done.37 = bf16[256,1536]{1,0:T(8,128)(2,1)S(1)} collective-permute-done((bf16[256,1536]{1,0:T(8,128)(2,1)}, bf16[256,1536]{1,0:T(8,128)(2,1)S(1)}, u32[]{:S(2)}, u32[]{:S(2)}) %collective-permute-start.37) | collective-permute-done | bytes 786464 | tf_op jit(solution)/shard_map/ppermute | solution.py:32
  275.7 3.2 fusion.24
  280.4 9.0 %shard_map.210 = (bf16[256,1536]{1,0:T(8,128)(2,1)}, bf16[256,1536]{1,0:T(8,128)(2,1)}, bf16[256,1536]{1,0:T(8,128)(2,1)}, bf16[128,1536]{1,0:T(8,128)(2,1)}, bf16[128,1536]{1,0:T(8,128)(2,1)}) custom-call(s32[1]{0:T(128)} %bitcast.6.z_ref, bf16[2,1024,512]{2,1,0:T(8,128)(2,1)} %get-tuple-element.173.hidden.left, ...), custom_call_target="tpu_custom_call" | custom-call | flops 966367616 | bytes 2400000 | tf_op jit(solution)/shard_map/pallas_call | solution.py:573
  289.4 5.7 %shard_map.214 = bf16[512,1536]{1,0:T(8,128)(2,1)} custom-call(bf16[2,1024,512]{2,1,0:T(8,128)(2,1)} %get-tuple-element.173.hidden.left, bf16[1024,1536]{1,0:T(8,128)(2,1)} %get-tuple-element.183.right, bf16[512,1536]{1,0:T(8,128)(2,1)} %collective-permute-done.41.rest_0_), custom_call_target="tpu_custom_call" | custom-call | flops 483183808 | bytes 3000000 | tf_op jit(solution)/shard_map/pallas_call | solution.py:611
  301.6 17.0 %shard_map.215 = (bf16[2,512,384]{2,1,0:T(8,128)(2,1)}, f32[2,512,256]{2,1,0:T(8,128)}, bf16[512,384]{1,0:T(8,128)(2,1)}, bf16[2,192,1536]{2,1,0:T(8,128)(2,1)}) custom-call(s32[1]{0:T(128)} %bitcast.y_ref.refs_0_, bf16[2,512,384]{2,1,0:T(8,128)(2,1)} %get-tuple-element.153.qkv.refs_1_, bf16[512,384]{1,0:T(8,128)(2,1)} %collective-permute-done.9.halo.refs_2_, ...), custom_call_target="tpu_custom_call" | custom-call | flops 3600000000 | bytes 3000000 | tf_op jit(solution)/shard_map/pallas_call | solution.py:744
  320.6 17.5 %shard_map.216 = (bf16[2,512,384]{2,1,0:T(8,128)(2,1)}, f32[2,512,256]{2,1,0:T(8,128)}, bf16[512,384]{1,0:T(8,128)(2,1)}, bf16[2,192,1536]{2,1,0:T(8,128)(2,1)}) custom-call(s32[1]{0:T(128)} %bitcast.y_ref.refs_0_, bf16[2,512,384]{2,1,0:T(8,128)(2,1)} %get-tuple-element.165.qkv.refs_1_, bf16[512,384]{1,0:T(8,128)(2,1)} %copy-done.58, ...), custom_call_target="tpu_custom_call" | custom-call | flops 3600000000 | bytes 3000000 | tf_op jit(solution)/shard_map/pallas_call | solution.py:744
  355.5 7.0 %collective-permute-done.49.grad_halo = bf16[512,384]{1,0:T(8,128)(2,1)} collective-permute-done((bf16[512,384]{1,0:T(8,128)(2,1)}, bf16[512,384]{1,0:T(8,128)(2,1)}, u32[]{:S(2)}, u32[]{:S(2)}) %collective-permute-start.49) | collective-permute-done | bytes 393248 | tf_op jit(solution)/shard_map/ppermute | solution.py:32
  362.5 4.6 all-to-all-start.3
  367.1 7.0 %shard_map.218 = (bf16[2,512,384]{2,1,0:T(8,128)(2,1)}, bf16[256,1536]{1,0:T(8,128)(2,1)}, bf16[128,1536]{1,0:T(8,128)(2,1)}, bf16[128,1536]{1,0:T(8,128)(2,1)}) custom-call(bf16[2,512,384]{2,1,0:T(8,128)(2,1)} %get-tuple-element.212.grad_query, f32[2,512,256]{2,1,0:T(8,128)} %get-tuple-element.213.grad_kv, ...), custom_call_target="tpu_custom_call" | custom-call | flops 362387872 | bytes 1800000 | tf_op jit(solution)/shard_map/pallas_call | solution.py:816
  374.1 3.4 fusion.6
  377.5 6.9 %shard_map.217 = (bf16[2,512,384]{2,1,0:T(8,128)(2,1)}, bf16[256,1536]{1,0:T(8,128)(2,1)}, bf16[256,1536]{1,0:T(8,128)(2,1)}) custom-call(bf16[2,512,384]{2,1,0:T(8,128)(2,1)} %get-tuple-element.208.grad_query, f32[2,512,256]{2,1,0:T(8,128)} %get-tuple-element.209.grad_kv, bf16[512,384]{1,0:T(8,128)(2,1)} %collective-permute-done.48.grad_halo, ...), custom_call_target="tpu_custom_call" | custom-call | flops 362387872 | bytes 1800000 | tf_op jit(solution)/shard_map/pallas_call | solution.py:816
  384.4 3.3 fusion.1
  400.1 4.1 all-to-all-start.2
  409.5 12.1 %collective-permute-done.51 = bf16[128,1536]{1,0:T(8,128)(2,1)S(1)} collective-permute-done((bf16[128,1536]{1,0:T(8,128)(2,1)}, bf16[128,1536]{1,0:T(8,128)(2,1)S(1)}, u32[]{:S(2)}, u32[]{:S(2)}) %collective-permute-start.51) | collective-permute-done | bytes 393248 | tf_op jit(solution)/shard_map/ppermute | solution.py:32
  427.1 2.9 add_convert_fusion.1
  430.0 7.0 %collective-permute-done.61 = bf16[384,1024]{1,0:T(8,128)(2,1)} collective-permute-done((bf16[384,1024]{1,0:T(8,128)(2,1)}, bf16[384,1024]{1,0:T(8,128)(2,1)}, u32[]{:S(2)}, u32[]{:S(2)}) %collective-permute-start.61) | collective-permute-done | bytes 786464 | tf_op jit(solution)/shard_map/ppermute | solution.py:32
  440.6 4.0 all-to-all-done.2
  446.8 7.1 %collective-permute-done.53 = bf16[256,1536]{1,0:T(8,128)(2,1)} collective-permute-done((bf16[256,1536]{1,0:T(8,128)(2,1)}, bf16[256,1536]{1,0:T(8,128)(2,1)}, u32[]{:S(2)}, u32[]{:S(2)}) %collective-permute-start.53) | collective-permute-done | bytes 786464 | tf_op jit(solution)/shard_map/ppermute | solution.py:32
  457.0 4.0 collective-permute-done.64.b2
  463.5 13.8 %collective-permute-start.59 = (bf16[576,384]{1,0:T(8,128)(2,1)}, bf16[576,384]{1,0:T(8,128)(2,1)}, u32[]{:S(2)}, u32[]{:S(2)}) collective-permute-start(bf16[576,384]{1,0:T(8,128)(2,1)} %pad_maximum_fusion.11.refs_0_), channel_id=1, source_target_pairs={{0,16},{1,17},{2,18},{3,19},{4,20},{5,21},{6,22},{7,23},{8,24},{9,... | collective-permute-start | bytes 1327112 | tf_op jit(solution)/shard_map/ppermute | solution.py:32
  477.4 6.5 %shard_map.219 = (f32[192,4096]{1,0:T(8,128)}, f32[192,4096]{1,0:T(8,128)}, f32[192,1]{1,0:T(8,128)}) custom-call(s32[1]{0:T(128)} %bitcast.1.d_ref, bf16[2,192,1024]{2,1,0:T(8,128)(2,1)} %pad_maximum_fusion.7.refs_0_, bf16[2,192,1024]{2,1,0:T(8,128)(2,1)} %bitcast.40.refs_1_, bf16[2,192,1024]{2,1,0:T(8,128)(2,1)} %bitcast.41.refs_2_, ...), custom_call_target="tpu_custom_call" | custom-call | flops 1415577 | bytes 3774873 | tf_op jit(solution)/shard_map/pallas_call | solution.py:848
  484.6 3.3 shard_map.220
  488.5 3.2 fusion.4
  492.3 5.2 %shard_map.221 = (f32[192,1536]{1,0:T(8,128)}, f32[192,768]{1,0:T(8,128)}, f32[192,768]{1,0:T(8,128)}, f32[192,1536]{1,0:T(8,128)}, f32[192,1]{1,0:T(8,128)}) custom-call(s32[1]{0:T(128)} %bitcast.1.d_ref, bf16[576,384]{1,0:T(8,128)(2,1)} %pad_maximum_fusion.11.refs_0_, bf16[576,384]{1,0:T(8,128)(2,1)} %collective-permute-done.58.refs_1_, ...), custom_call_target="tpu_custom_call" | custom-call | flops 1200000000 | bytes 2400000 | tf_op jit(solution)/shard_map/pallas_call | solution.py:927
  (376 shorter events, 133.5 us)
Async XLA Ops:
  0.7 43.2 %collective-permute-start.3 = (s32[1,8]{1,0:T(1,128)}, s32[1,8]{1,0:T(1,128)S(1)}, u32[]{:S(2)}, u32[]{:S(2)}) collective-permute-start(s32[1,8]{1,0:T(1,128)} %param.21), channel_id=1, source_target_pairs={{0,16},{1,17},{2,18},{3,19},{4,20},{5,21},{6,22},{7,23},{8,24},{9,... | collective-permute-start | bytes 104 | tf_op jit(solution)/shard_map/ppermute | solution.py:32
  9.2 19.0 %collective-permute-start.4 = (bf16[256,1536]{1,0:T(8,128)(2,1)}, bf16[256,1536]{1,0:T(8,128)(2,1)}, u32[]{:S(2)}, u32[]{:S(2)}) collective-permute-start(bf16[256,1536]{1,0:T(8,128)(2,1)} %refs_0_.1), channel_id=1, source_target_pairs={{0,16},{1,17},{2,18},{3,19},{4,20},{5,21},{6,22},{7,23},{8,24},{9,... | collective-permute-start | bytes 2359304 | tf_op jit(solution)/shard_map/ppermute | solution.py:32
  13.5 24.6 %collective-permute-start.1 = (bf16[256,1536]{1,0:T(8,128)(2,1)S(1)}, bf16[256,1536]{1,0:T(8,128)(2,1)}, u32[]{:S(2)}, u32[]{:S(2)}) collective-permute-start(bf16[256,1536]{1,0:T(8,128)(2,1)S(1)} %copy-done.5), channel_id=1, source_target_pairs={{0,1},{1,0},{2,3},{3,2},{4,5},{5,4},{6,7},{7,6},{8,9},{9,8},{10,11... | collective-permute-start | bytes 2359304 | tf_op jit(solution)/shard_map/ppermute | solution.py:32
  16.3 40.1 %all-to-all-start = ((bf16[4,400,384]{2,1,0:T(8,128)(2,1)}), bf16[4,400,384]{2,1,0:T(8,128)(2,1)S(1)}, u32[]{:S(2)}, u32[]{:S(2)}) async-start(bf16[4,400,384]{2,1,0:T(8,128)(2,1)} %broadcast_in_dim.66), calls=%async_computation | async-start | bytes 2457600 | tf_op jit(solution)/shard_map/all_to_all | solution.py:100
  32.1 24.3 %collective-permute-start.6 = (bf16[48,1536]{1,0:T(8,128)(2,1)}, bf16[48,1536]{1,0:T(8,128)(2,1)}, u32[]{:S(2)}, u32[]{:S(2)}) collective-permute-start(bf16[48,1536]{1,0:T(8,128)(2,1)} %constant_dynamic-slice_fusion.3), channel_id=1, source_target_pairs={{0,0},{1,1},{2,8},{3,9},{4,16},{5,17},{6,24},{7,25},{8,2},{9,3},{1... | collective-permute-start | bytes 442376 | tf_op jit(solution)/shard_map/ppermute | solution.py:32
  39.1 17.2 %collective-permute-start.7 = (bf16[128,1536]{1,0:T(8,128)(2,1)S(1)}, bf16[128,1536]{1,0:T(8,128)(2,1)S(1)}, u32[]{:S(2)}, u32[]{:S(2)}) collective-permute-start(bf16[128,1536]{1,0:T(8,128)(2,1)S(1)} %slice.390), channel_id=1, source_target_pairs={{0,16},{1,17},{2,18},{3,19},{4,20},{5,21},{6,22},{7,23},{8,24},{9,... | collective-permute-start | bytes 1179656 | tf_op jit(solution)/shard_map/ppermute | solution.py:32
  57.2 28.0 %collective-permute-start.11 = (bf16[256,1536]{1,0:T(8,128)(2,1)}, bf16[256,1536]{1,0:T(8,128)(2,1)}, u32[]{:S(2)}, u32[]{:S(2)}) collective-permute-start(bf16[256,1536]{1,0:T(8,128)(2,1)} %refs_5_.3), channel_id=1, source_target_pairs={{0,1},{1,0},{2,3},{3,2},{4,5},{5,4},{6,7},{7,6},{8,9},{9,8},{10,11... | collective-permute-start | bytes 2359304 | tf_op jit(solution)/shard_map/ppermute | solution.py:32
  58.7 26.5 %collective-permute-start.10 = (bf16[256,1536]{1,0:T(8,128)(2,1)}, bf16[256,1536]{1,0:T(8,128)(2,1)}, u32[]{:S(2)}, u32[]{:S(2)}) collective-permute-start(bf16[256,1536]{1,0:T(8,128)(2,1)} %refs_5_.3), channel_id=1, source_target_pairs={{0,16},{1,17},{2,18},{3,19},{4,20},{5,21},{6,22},{7,23},{8,24},{9,... | collective-permute-start | bytes 2359304 | tf_op jit(solution)/shard_map/ppermute | solution.py:32
  59.9 18.1 %collective-permute-start.16 = (bf16[48,1536]{1,0:T(8,128)(2,1)}, bf16[48,1536]{1,0:T(8,128)(2,1)S(1)}, u32[]{:S(2)}, u32[]{:S(2)}) collective-permute-start(bf16[48,1536]{1,0:T(8,128)(2,1)} %collective-permute-done.6), channel_id=1, source_target_pairs={{0,6},{1,7},{2,4},{3,5},{4,2},{5,3},{6,0},{7,1},{8,14},{9,15},{10,... | collective-permute-start | bytes 442376 | tf_op jit(solution)/shard_map/ppermute | solution.py:32
  59.9 18.1 %collective-permute-start.15 = (bf16[48,1536]{1,0:T(8,128)(2,1)}, bf16[48,1536]{1,0:T(8,128)(2,1)S(1)}, u32[]{:S(2)}, u32[]{:S(2)}) collective-permute-start(bf16[48,1536]{1,0:T(8,128)(2,1)} %collective-permute-done.6), channel_id=1, source_target_pairs={{0,4},{1,5},{2,6},{3,7},{4,0},{5,1},{6,2},{7,3},{8,12},{9,13},{10,... | collective-permute-start | bytes 442376 | tf_op jit(solution)/shard_map/ppermute | solution.py:32
  60.0 17.9 %collective-permute-start.14 = (bf16[48,1536]{1,0:T(8,128)(2,1)}, bf16[48,1536]{1,0:T(8,128)(2,1)S(1)}, u32[]{:S(2)}, u32[]{:S(2)}) collective-permute-start(bf16[48,1536]{1,0:T(8,128)(2,1)} %collective-permute-done.6), channel_id=1, source_target_pairs={{0,2},{1,3},{2,0},{3,1},{4,6},{5,7},{6,4},{7,5},{8,10},{9,11},{10,... | collective-permute-start | bytes 442376 | tf_op jit(solution)/shard_map/ppermute | solution.py:32
  82.2 24.5 %collective-permute-start.9 = (bf16[512,384]{1,0:T(8,128)(2,1)}, bf16[512,384]{1,0:T(8,128)(2,1)}, u32[]{:S(2)}, u32[]{:S(2)}) collective-permute-start(bf16[512,384]{1,0:T(8,128)(2,1)} %get-tuple-element.154), channel_id=1, source_target_pairs={{0,2},{1,3},{2,4},{3,5},{4,6},{5,7},{8,10},{9,11},{10,12},{11,13},... | collective-permute-start | bytes 1179656 | tf_op jit(solution)/shard_map/ppermute | solution.py:32
  87.3 19.5 %collective-permute-start.12 = (bf16[128,1536]{1,0:T(8,128)(2,1)S(1)}, bf16[128,1536]{1,0:T(8,128)(2,1)}, u32[]{:S(2)}, u32[]{:S(2)}) collective-permute-start(bf16[128,1536]{1,0:T(8,128)(2,1)S(1)} %slice.315), channel_id=1, source_target_pairs={{0,1},{1,0},{2,3},{3,2},{4,5},{5,4},{6,7},{7,6},{8,9},{9,8},{10,11... | collective-permute-start | bytes 1179656 | tf_op jit(solution)/shard_map/ppermute | solution.py:32
  87.8 19.0 %collective-permute-start.13 = (bf16[128,1536]{1,0:T(8,128)(2,1)S(1)}, bf16[128,1536]{1,0:T(8,128)(2,1)}, u32[]{:S(2)}, u32[]{:S(2)}) collective-permute-start(bf16[128,1536]{1,0:T(8,128)(2,1)S(1)} %slice.316), channel_id=1, source_target_pairs={{0,16},{1,17},{2,18},{3,19},{4,20},{5,21},{6,22},{7,23},{8,24},{9,... | collective-permute-start | bytes 1179656 | tf_op jit(solution)/shard_map/ppermute | solution.py:32
  106.7 53.5 %collective-permute-start.24 = (bf16[576,1024]{1,0:T(8,128)(2,1)S(1)}, bf16[576,1024]{1,0:T(8,128)(2,1)S(1)}, u32[]{:S(2)}, u32[]{:S(2)}) collective-permute-start(bf16[576,1024]{1,0:T(8,128)(2,1)S(1)} %copy-done.10), channel_id=1, source_target_pairs={{0,2},{1,3},{2,0},{3,1},{4,6},{5,7},{6,4},{7,5},{8,10},{9,11},{10,... | collective-permute-start | bytes 3538952 | tf_op jit(solution)/shard_map/ppermute | solution.py:32
  106.7 53.5 %collective-permute-start.23 = (bf16[576,1024]{1,0:T(8,128)(2,1)S(1)}, bf16[576,1024]{1,0:T(8,128)(2,1)}, u32[]{:S(2)}, u32[]{:S(2)}) collective-permute-start(bf16[576,1024]{1,0:T(8,128)(2,1)S(1)} %copy-done.10), channel_id=1, source_target_pairs={{0,4},{1,5},{2,6},{3,7},{4,0},{5,1},{6,2},{7,3},{8,12},{9,13},{10,... | collective-permute-start | bytes 3538952 | tf_op jit(solution)/shard_map/ppermute | solution.py:32
  123.5 36.7 %collective-permute-start.20 = (bf16[256,1536]{1,0:T(8,128)(2,1)}, bf16[256,1536]{1,0:T(8,128)(2,1)}, u32[]{:S(2)}, u32[]{:S(2)}) collective-permute-start(bf16[256,1536]{1,0:T(8,128)(2,1)} %pad_maximum_fusion.1), channel_id=1, source_target_pairs={{0,16},{1,17},{2,18},{3,19},{4,20},{5,21},{6,22},{7,23},{8,24},{9,... | collective-permute-start | bytes 2359304 | tf_op jit(solution)/shard_map/ppermute | solution.py:32
  126.5 33.8 %collective-permute-start.22 = (bf16[256,1536]{1,0:T(8,128)(2,1)}, bf16[256,1536]{1,0:T(8,128)(2,1)}, u32[]{:S(2)}, u32[]{:S(2)}) collective-permute-start(bf16[256,1536]{1,0:T(8,128)(2,1)} %pad_maximum_fusion.2), channel_id=1, source_target_pairs={{0,1},{1,0},{2,3},{3,2},{4,5},{5,4},{6,7},{7,6},{8,9},{9,8},{10,11... | collective-permute-start | bytes 2359304 | tf_op jit(solution)/shard_map/ppermute | solution.py:32
  160.2 26.4 %collective-permute-start.29 = (bf16[576,1024]{1,0:T(8,128)(2,1)}, bf16[576,1024]{1,0:T(8,128)(2,1)S(1)}, u32[]{:S(2)}, u32[]{:S(2)}) collective-permute-start(bf16[576,1024]{1,0:T(8,128)(2,1)} %collective-permute-done.23.refs_12_.refs_2_), channel_id=1, source_target_pairs={{0,2},{1,3},{2,0},{3,1},{4,6},{5,7},{6,4},{7,5},{8,10},{9,11},{10,... | collective-permute-start | bytes 3538952 | tf_op jit(solution)/shard_map/ppermute | solution.py:32
  164.5 17.8 %collective-permute-start.26 = (bf16[256,1536]{1,0:T(8,128)(2,1)S(1)}, bf16[256,1536]{1,0:T(8,128)(2,1)S(1)}, u32[]{:S(2)}, u32[]{:S(2)}) collective-permute-start(bf16[256,1536]{1,0:T(8,128)(2,1)S(1)} %multiply_convert_fusion.refs_0_), channel_id=1, source_target_pairs={{0,16},{1,17},{2,18},{3,19},{4,20},{5,21},{6,22},{7,23},{8,24},{9,... | collective-permute-start | bytes 2359304 | tf_op jit(solution)/shard_map/ppermute | solution.py:32
  165.7 21.2 %collective-permute-start.30 = (bf16[576,1024]{1,0:T(8,128)(2,1)S(1)}, bf16[576,1024]{1,0:T(8,128)(2,1)S(1)}, u32[]{:S(2)}, u32[]{:S(2)}) collective-permute-start(bf16[576,1024]{1,0:T(8,128)(2,1)S(1)} %copy-done.10), channel_id=1, source_target_pairs={{0,8},{1,9},{2,10},{3,11},{4,12},{5,13},{6,14},{7,15},{8,0},{9,1},... | collective-permute-start | bytes 3538952 | tf_op jit(solution)/shard_map/ppermute | solution.py:32
  165.7 22.4 %collective-permute-start.31 = (bf16[576,1024]{1,0:T(8,128)(2,1)S(1)}, bf16[576,1024]{1,0:T(8,128)(2,1)S(1)}, u32[]{:S(2)}, u32[]{:S(2)}) collective-permute-start(bf16[576,1024]{1,0:T(8,128)(2,1)S(1)} %copy-done.18), channel_id=1, source_target_pairs={{0,8},{1,9},{2,10},{3,11},{4,12},{5,13},{6,14},{7,15},{8,0},{9,1},... | collective-permute-start | bytes 3538952 | tf_op jit(solution)/shard_map/ppermute | solution.py:32
  166.2 20.5 %collective-permute-start.25 = (bf16[256,1536]{1,0:T(8,128)(2,1)S(1)}, bf16[256,1536]{1,0:T(8,128)(2,1)S(1)}, u32[]{:S(2)}, u32[]{:S(2)}) collective-permute-start(bf16[256,1536]{1,0:T(8,128)(2,1)S(1)} %multiply_convert_fusion.refs_0_), channel_id=1, source_target_pairs={{0,1},{1,0},{2,3},{3,2},{4,5},{5,4},{6,7},{7,6},{8,9},{9,8},{10,11... | collective-permute-start | bytes 2359304 | tf_op jit(solution)/shard_map/ppermute | solution.py:32
  252.7 19.6 %collective-permute-start.37 = (bf16[256,1536]{1,0:T(8,128)(2,1)}, bf16[256,1536]{1,0:T(8,128)(2,1)S(1)}, u32[]{:S(2)}, u32[]{:S(2)}) collective-permute-start(bf16[256,1536]{1,0:T(8,128)(2,1)} %pad_maximum_fusion.3), channel_id=1, source_target_pairs={{0,16},{1,17},{2,18},{3,19},{4,20},{5,21},{6,22},{7,23},{8,24},{9,... | collective-permute-start | bytes 2359304 | tf_op jit(solution)/shard_map/ppermute | solution.py:32
  254.5 19.4 %collective-permute-start.38 = (bf16[256,1536]{1,0:T(8,128)(2,1)}, bf16[256,1536]{1,0:T(8,128)(2,1)}, u32[]{:S(2)}, u32[]{:S(2)}) collective-permute-start(bf16[256,1536]{1,0:T(8,128)(2,1)} %pad_maximum_fusion.4), channel_id=1, source_target_pairs={{0,1},{1,0},{2,3},{3,2},{4,5},{5,4},{6,7},{7,6},{8,9},{9,8},{10,11... | collective-permute-start | bytes 2359304 | tf_op jit(solution)/shard_map/ppermute | solution.py:32
  254.8 34.5 %collective-permute-start.41 = (bf16[512,1536]{1,0:T(8,128)(2,1)}, bf16[512,1536]{1,0:T(8,128)(2,1)}, u32[]{:S(2)}, u32[]{:S(2)}) collective-permute-start(bf16[512,1536]{1,0:T(8,128)(2,1)} %shard_map.211), channel_id=1, source_target_pairs={{0,8},{1,9},{2,10},{3,11},{4,12},{5,13},{6,14},{7,15},{8,0},{9,1},... | collective-permute-start | bytes 4718600 | tf_op jit(solution)/shard_map/ppermute | solution.py:32
  254.8 88.9 %all-to-all-start.1 = ((bf16[4,384,1024]{2,1,0:T(8,128)(2,1)}), bf16[4,384,1024]{2,1,0:T(8,128)(2,1)}, u32[]{:S(2)}, u32[]{:S(2)}) async-start(bf16[4,384,1024]{2,1,0:T(8,128)(2,1)} %bitcast.86), calls=%async_computation.1 | async-start | bytes 6291456 | tf_op jit(solution)/shard_map/all_to_all | solution.py:100
  278.9 18.4 %collective-permute-start.40 = (bf16[256,1536]{1,0:T(8,128)(2,1)}, bf16[256,1536]{1,0:T(8,128)(2,1)S(1)}, u32[]{:S(2)}, u32[]{:S(2)}) collective-permute-start(bf16[256,1536]{1,0:T(8,128)(2,1)} %get-tuple-element.189.refs_10_), channel_id=1, source_target_pairs={{0,1},{1,0},{2,3},{3,2},{4,5},{5,4},{6,7},{7,6},{8,9},{9,8},{10,11... | collective-permute-start | bytes 2359304 | tf_op jit(solution)/shard_map/ppermute | solution.py:32
  279.2 18.1 %collective-permute-start.39 = (bf16[256,1536]{1,0:T(8,128)(2,1)}, bf16[256,1536]{1,0:T(8,128)(2,1)S(1)}, u32[]{:S(2)}, u32[]{:S(2)}) collective-permute-start(bf16[256,1536]{1,0:T(8,128)(2,1)} %get-tuple-element.189.refs_10_), channel_id=1, source_target_pairs={{0,16},{1,17},{2,18},{3,19},{4,20},{5,21},{6,22},{7,23},{8,24},{9,... | collective-permute-start | bytes 2359304 | tf_op jit(solution)/shard_map/ppermute | solution.py:32
  299.3 19.3 %collective-permute-start.42 = (bf16[128,1536]{1,0:T(8,128)(2,1)S(1)}, bf16[128,1536]{1,0:T(8,128)(2,1)S(1)}, u32[]{:S(2)}, u32[]{:S(2)}) collective-permute-start(bf16[128,1536]{1,0:T(8,128)(2,1)S(1)} %slice.329), channel_id=1, source_target_pairs={{0,1},{1,0},{2,3},{3,2},{4,5},{5,4},{6,7},{7,6},{8,9},{9,8},{10,11... | collective-permute-start | bytes 1179656 | tf_op jit(solution)/shard_map/ppermute | solution.py:32
  300.5 18.2 %collective-permute-start.43 = (bf16[128,1536]{1,0:T(8,128)(2,1)S(1)}, bf16[128,1536]{1,0:T(8,128)(2,1)}, u32[]{:S(2)}, u32[]{:S(2)}) collective-permute-start(bf16[128,1536]{1,0:T(8,128)(2,1)S(1)} %slice.330), channel_id=1, source_target_pairs={{0,16},{1,17},{2,18},{3,19},{4,20},{5,21},{6,22},{7,23},{8,24},{9,... | collective-permute-start | bytes 1179656 | tf_op jit(solution)/shard_map/ppermute | solution.py:32
  318.7 29.6 %collective-permute-start.44 = (bf16[128,1536]{1,0:T(8,128)(2,1)}, bf16[128,1536]{1,0:T(8,128)(2,1)}, u32[]{:S(2)}, u32[]{:S(2)}) collective-permute-start(bf16[128,1536]{1,0:T(8,128)(2,1)} %get-tuple-element.201), channel_id=1, source_target_pairs={{0,1},{1,0},{2,3},{3,2},{4,5},{5,4},{6,7},{7,6},{8,9},{9,8},{10,11... | collective-permute-start | bytes 1179656 | tf_op jit(solution)/shard_map/ppermute | solution.py:32
  319.7 28.6 %collective-permute-start.45 = (bf16[128,1536]{1,0:T(8,128)(2,1)}, bf16[128,1536]{1,0:T(8,128)(2,1)}, u32[]{:S(2)}, u32[]{:S(2)}) collective-permute-start(bf16[128,1536]{1,0:T(8,128)(2,1)} %get-tuple-element.202), channel_id=1, source_target_pairs={{0,16},{1,17},{2,18},{3,19},{4,20},{5,21},{6,22},{7,23},{8,24},{9,... | collective-permute-start | bytes 1179656 | tf_op jit(solution)/shard_map/ppermute | solution.py:32
  351.0 26.5 %collective-permute-start.48 = (bf16[512,384]{1,0:T(8,128)(2,1)}, bf16[512,384]{1,0:T(8,128)(2,1)}, u32[]{:S(2)}, u32[]{:S(2)}) collective-permute-start(bf16[512,384]{1,0:T(8,128)(2,1)} %get-tuple-element.210), channel_id=1, source_target_pairs={{2,0},{3,1},{4,2},{5,3},{6,4},{7,5},{10,8},{11,9},{12,10},{13,11},... | collective-permute-start | bytes 1179656 | tf_op jit(solution)/shard_map/ppermute | solution.py:32
  362.5 37.6 %all-to-all-start.3 = ((bf16[4,128,1536]{2,1,0:T(8,128)(2,1)}), bf16[4,128,1536]{2,1,0:T(8,128)(2,1)}, u32[]{:S(2)}, u32[]{:S(2)}) async-start(bf16[4,128,1536]{2,1,0:T(8,128)(2,1)} %bitcast.44), calls=%async_computation.3 | async-start | bytes 3145728 | tf_op jit(solution)/shard_map/all_to_all | solution.py:100
  391.0 30.6 %collective-permute-start.46 = (bf16[256,1536]{1,0:T(8,128)(2,1)}, bf16[256,1536]{1,0:T(8,128)(2,1)}, u32[]{:S(2)}, u32[]{:S(2)}) collective-permute-start(bf16[256,1536]{1,0:T(8,128)(2,1)} %pad_maximum_fusion.5), channel_id=1, source_target_pairs={{0,16},{1,17},{2,18},{3,19},{4,20},{5,21},{6,22},{7,23},{8,24},{9,... | collective-permute-start | bytes 2359304 | tf_op jit(solution)/shard_map/ppermute | solution.py:32
  394.1 27.5 %collective-permute-start.47 = (bf16[256,1536]{1,0:T(8,128)(2,1)}, bf16[256,1536]{1,0:T(8,128)(2,1)}, u32[]{:S(2)}, u32[]{:S(2)}) collective-permute-start(bf16[256,1536]{1,0:T(8,128)(2,1)} %pad_maximum_fusion.6), channel_id=1, source_target_pairs={{0,1},{1,0},{2,3},{3,2},{4,5},{5,4},{6,7},{7,6},{8,9},{9,8},{10,11... | collective-permute-start | bytes 2359304 | tf_op jit(solution)/shard_map/ppermute | solution.py:32
  400.1 44.5 %all-to-all-start.2 = ((bf16[4,576,384]{2,1,0:T(8,128)(2,1)}), bf16[4,576,384]{2,1,0:T(8,128)(2,1)S(1)}, u32[]{:S(2)}, u32[]{:S(2)}) async-start(bf16[4,576,384]{2,1,0:T(8,128)(2,1)} %add_convert_fusion), calls=%async_computation.2 | async-start | bytes 3538944 | tf_op jit(solution)/shard_map/all_to_all | solution.py:100
  404.2 17.4 %collective-permute-start.51 = (bf16[128,1536]{1,0:T(8,128)(2,1)}, bf16[128,1536]{1,0:T(8,128)(2,1)S(1)}, u32[]{:S(2)}, u32[]{:S(2)}) collective-permute-start(bf16[128,1536]{1,0:T(8,128)(2,1)} %get-tuple-element.217), channel_id=1, source_target_pairs={{0,1},{1,0},{2,3},{3,2},{4,5},{5,4},{6,7},{7,6},{8,9},{9,8},{10,11... | collective-permute-start | bytes 1179656 | tf_op jit(solution)/shard_map/ppermute | solution.py:32
  406.2 30.8 %collective-permute-start.61 = (bf16[384,1024]{1,0:T(8,128)(2,1)}, bf16[384,1024]{1,0:T(8,128)(2,1)}, u32[]{:S(2)}, u32[]{:S(2)}) collective-permute-start(bf16[384,1024]{1,0:T(8,128)(2,1)} %bitcast.89), channel_id=1, source_target_pairs={{0,16},{1,17},{2,18},{3,19},{4,20},{5,21},{6,22},{7,23},{8,24},{9,... | collective-permute-start | bytes 2359304 | tf_op jit(solution)/shard_map/ppermute | solution.py:32
  422.6 31.2 %collective-permute-start.53 = (bf16[256,1536]{1,0:T(8,128)(2,1)}, bf16[256,1536]{1,0:T(8,128)(2,1)}, u32[]{:S(2)}, u32[]{:S(2)}) collective-permute-start(bf16[256,1536]{1,0:T(8,128)(2,1)} %pad_maximum_fusion.8), channel_id=1, source_target_pairs={{0,16},{1,17},{2,18},{3,19},{4,20},{5,21},{6,22},{7,23},{8,24},{9,... | collective-permute-start | bytes 2359304 | tf_op jit(solution)/shard_map/ppermute | solution.py:32
  424.6 30.2 %collective-permute-start.54 = (bf16[256,1536]{1,0:T(8,128)(2,1)}, bf16[256,1536]{1,0:T(8,128)(2,1)}, u32[]{:S(2)}, u32[]{:S(2)}) collective-permute-start(bf16[256,1536]{1,0:T(8,128)(2,1)} %pad_maximum_fusion.9), channel_id=1, source_target_pairs={{0,1},{1,0},{2,3},{3,2},{4,5},{5,4},{6,7},{7,6},{8,9},{9,8},{10,11... | collective-permute-start | bytes 2359304 | tf_op jit(solution)/shard_map/ppermute | solution.py:32
  427.1 50.3 %collective-permute-start.60 = (bf16[384,1024]{1,0:T(8,128)(2,1)}, bf16[384,1024]{1,0:T(8,128)(2,1)}, u32[]{:S(2)}, u32[]{:S(2)}) collective-permute-start(bf16[384,1024]{1,0:T(8,128)(2,1)} %bitcast.90), channel_id=1, source_target_pairs={{0,8},{1,9},{2,10},{3,11},{4,12},{5,13},{6,14},{7,15},{8,0},{9,1},... | collective-permute-start | bytes 2359304 | tf_op jit(solution)/shard_map/ppermute | solution.py:32
  437.0 40.3 %collective-permute-start.62 = (bf16[384,1024]{1,0:T(8,128)(2,1)}, bf16[384,1024]{1,0:T(8,128)(2,1)}, u32[]{:S(2)}, u32[]{:S(2)}) collective-permute-start(bf16[384,1024]{1,0:T(8,128)(2,1)} %collective-permute-done.61), channel_id=1, source_target_pairs={{0,8},{1,9},{2,10},{3,11},{4,12},{5,13},{6,14},{7,15},{8,0},{9,1},... | collective-permute-start | bytes 2359304 | tf_op jit(solution)/shard_map/ppermute | solution.py:32
  439.5 21.4 %collective-permute-start.64 = (bf16[128,1536]{1,0:T(8,128)(2,1)}, bf16[128,1536]{1,0:T(8,128)(2,1)}, u32[]{:S(2)}, u32[]{:S(2)}) collective-permute-start(bf16[128,1536]{1,0:T(8,128)(2,1)} %reduce_sum.101.b0), channel_id=1, source_target_pairs={{0,16},{1,17},{2,18},{3,19},{4,20},{5,21},{6,22},{7,23},{8,24},{9,... | collective-permute-start | bytes 1179656 | tf_op jit(solution)/shard_map/ppermute | solution.py:32
  456.9 27.0 %collective-permute-start.63 = (bf16[128,1536]{1,0:T(8,128)(2,1)S(1)}, bf16[128,1536]{1,0:T(8,128)(2,1)S(1)}, u32[]{:S(2)}, u32[]{:S(2)}) collective-permute-start(bf16[128,1536]{1,0:T(8,128)(2,1)S(1)} %copy-done.15), channel_id=1, source_target_pairs={{0,8},{1,9},{2,10},{3,11},{4,12},{5,13},{6,14},{7,15},{8,0},{9,1},... | collective-permute-start | bytes 1179656 | tf_op jit(solution)/shard_map/ppermute | solution.py:32
  460.9 23.0 %collective-permute-start.65 = (bf16[128,1536]{1,0:T(8,128)(2,1)}, bf16[128,1536]{1,0:T(8,128)(2,1)}, u32[]{:S(2)}, u32[]{:S(2)}) collective-permute-start(bf16[128,1536]{1,0:T(8,128)(2,1)} %collective-permute-done.64.b2), channel_id=1, source_target_pairs={{0,8},{1,9},{2,10},{3,11},{4,12},{5,13},{6,14},{7,15},{8,0},{9,1},... | collective-permute-start | bytes 1179656 | tf_op jit(solution)/shard_map/ppermute | solution.py:32
  463.5 24.4 %collective-permute-start.59 = (bf16[576,384]{1,0:T(8,128)(2,1)}, bf16[576,384]{1,0:T(8,128)(2,1)}, u32[]{:S(2)}, u32[]{:S(2)}) collective-permute-start(bf16[576,384]{1,0:T(8,128)(2,1)} %pad_maximum_fusion.11.refs_0_), channel_id=1, source_target_pairs={{0,16},{1,17},{2,18},{3,19},{4,20},{5,21},{6,22},{7,23},{8,24},{9,... | collective-permute-start | bytes 1327112 | tf_op jit(solution)/shard_map/ppermute | solution.py:32
  (88 other events, 702.8 us)
where the time goes:
time: 509 us; the launch traced here: 500 us
  Pallas kernels  166 us (33%)
  waiting for transfers between devices  140 us (28%)
  starting transfers between devices  92.8 us (18%)
  other arithmetic  55.8 us (11%)
  local copies, waits for them, and re-layouts  33.5 us (7%)
  matrix products  8.78 us (2%)
    ppermute x67, waiting for transfers between devices, send(): return lax.ppermute(block, BOTH, route)  135 us
    ppermute x67, starting transfers between devices, send(): return lax.ppermute(block, BOTH, route)  74.6 us
    pallas_call x2, Pallas kernels, attend_back(): call(functools.partial(attend_back_kernel, len(upstream)), [shaped((slots...  34.5 us
    pallas_call x1, Pallas kernels, feed_forward(): call(functools.partial(mlp_kernel, n_z), [shaped((2, tokens, ff), BF), sh...  27.1 us
    pallas_call x4, Pallas kernels, weight_grads(): call(grads_kernel, shaped((rows, columns), BF), flops=2 * tokens * rows *...  25.9 us
    pallas_call x2, Pallas kernels, attend(): call(attend_kernel, [shaped((size, width), BF) for size in sizes] + [shap...  22.7 us
    all_to_all x4, starting transfers between devices, along_z(): return lax.all_to_all(blocks, 'seq', 0, 0, axis_index_groups=lines)  18.3 us
    pallas_call x2, Pallas kernels, qkv_back(): call(qkv_back_kernel, outs, flops=2 * slots * tokens * width * lanes, mov...  13.9 us
  transfers between devices with their start and end apart: 71, of which 20 were waited for; matrix products, arithmetic and copies ran while one was open for 17% of the time, Pallas kernels for 25%

commit v1 on v0

--- a/solution.py
+++ b/solution.py
@@ -1089,7 +1089,7 @@
                 [blocks[:, : 2 * shard].reshape(width, -1), fold(down_rows, 2 * n_z * ff_part)], axis=0
             )
         ]
-    cotangent_in = after(cotangent, *tokens_all)
+    cotangent_in = after(cotangent, normed[1])
     came = (send(cotangent_in, across_x), send(cotangent_in, across_y))
     upstream_all = gather_plane(cotangent, *halo, came=came)
     halo_first = lax.optimization_barrier((halo_in[0], *upstream_all))[0]

time: 509 us -> 506 us (level)
  waiting for transfers between devices: 140 us -> 134 us
    ppermute x67, waiting for transfers between devices: 135 us -> 129 us  [send(): return lax.ppermute(block, BOTH, route)]
  transfers between devices with their start and end apart: 71 -> 71, of which waited for: 20 -> 24; matrix products, arithmetic and copies ran while one was open for 17% -> 17% of each run, Pallas kernels for 25% -> 26%
where the time goes in v1:
time: 506 us; the launch traced here: 496 us
  Pallas kernels  166 us (33%)
  waiting for transfers between devices  134 us (26%)
  starting transfers between devices  94.3 us (19%)
  other arithmetic  54.8 us (11%)
  local copies, waits for them, and re-layouts  35.1 us (7%)
  matrix products  8.79 us (2%)
    ppermute x67, waiting for transfers between devices, send(): return lax.ppermute(block, BOTH, route)  129 us
    ppermute x67, starting transfers between devices, send(): return lax.ppermute(block, BOTH, route)  76.2 us
    pallas_call x2, Pallas kernels, attend_back(): call(functools.partial(attend_back_kernel, len(upstream)), [shaped((slots...  34.5 us
    pallas_call x1, Pallas kernels, feed_forward(): call(functools.partial(mlp_kernel, n_z), [shaped((2, tokens, ff), BF), sh...  27.2 us
    pallas_call x4, Pallas kernels, weight_grads(): call(grads_kernel, shaped((rows, columns), BF), flops=2 * tokens * rows *...  25.9 us
    pallas_call x2, Pallas kernels, attend(): call(attend_kernel, [shaped((size, width), BF) for size in sizes] + [shap...  22.6 us
    all_to_all x4, starting transfers between devices, along_z(): return lax.all_to_all(blocks, 'seq', 0, 0, axis_index_groups=lines)  18 us
    pallas_call x2, Pallas kernels, qkv_back(): call(qkv_back_kernel, outs, flops=2 * slots * tokens * width * lanes, mov...  13.9 us
  transfers between devices with their start and end apart: 71, of which 24 were waited for; matrix products, arithmetic and copies ran while one was open for 17% of the time, Pallas kernels for 26%

profile of v1, /device:TPU:0, one launch (start us, length us, event | category | flops | bytes accessed | tf_op | source)
XLA Modules:
  0.0 496.3 jit_solution(4886887440092652065)
XLA Ops:
  0.7 3.0 collective-permute-start.3
  9.8 3.4 collective-permute-done
  16.3 4.9 all-to-all-start
  22.7 5.6 %collective-permute-done.4.refs_0_ = bf16[256,1536]{1,0:T(8,128)(2,1)} collective-permute-done((bf16[256,1536]{1,0:T(8,128)(2,1)}, bf16[256,1536]{1,0:T(8,128)(2,1)}, u32[]{:S(2)}, u32[]{:S(2)}) %collective-permute-start.4) | collective-permute-done | bytes 786464 | tf_op jit(solution)/shard_map/ppermute | solution.py:32
  35.1 3.0 shard_map.203
  39.1 3.2 collective-permute-start.7
  44.2 3.1 multiply_sine_fusion
  47.2 7.2 %collective-permute-done.2 = bf16[192,1024]{1,0:T(8,128)(2,1)S(1)} collective-permute-done((bf16[192,1024]{1,0:T(8,128)(2,1)}, bf16[192,1024]{1,0:T(8,128)(2,1)S(1)}, u32[]{:S(2)}, u32[]{:S(2)}) %collective-permute-start.2) | collective-permute-done | bytes 393248 | tf_op jit(solution)/shard_map/ppermute | solution.py:32
  57.3 4.3 collective-permute-start.14
  63.3 6.5 %shard_map.205 = (bf16[512,1536]{1,0:T(8,128)(2,1)}, bf16[2,512,384]{2,1,0:T(8,128)(2,1)}, bf16[512,384]{1,0:T(8,128)(2,1)}) custom-call(bf16[256,1536]{1,0:T(8,128)(2,1)} %collective-permute-done.4.refs_0_, bf16[128,1536]{1,0:T(8,128)(2,1)} %collective-permute-done.5.refs_1_, bf16[128,1536]{1,0:T(8,128)(2,1)} %copy-done.47, f32[1,1536]{1,0:T(1,128)} %bitcast.96, ...), custom_call_target="tpu_custom_call" | custom-call | flops 362387872 | bytes 1800000 | tf_op jit(solution)/shard_map/pallas_call | solution.py:269
  69.8 6.6 %shard_map.204 = (bf16[512,1536]{1,0:T(8,128)(2,1)}, bf16[2,512,384]{2,1,0:T(8,128)(2,1)}, bf16[512,384]{1,0:T(8,128)(2,1)}) custom-call(bf16[256,1536]{1,0:T(8,128)(2,1)} %refs_0_.1, bf16[256,1536]{1,0:T(8,128)(2,1)} %collective-permute-done.1.refs_1_, f32[1,1536]{1,0:T(1,128)} %bitcast.97, f32[1024,128]{1,0:T(8,128)} %get-tuple-element.302.refs_3_.refs_4_.refs_8_.cosine, ...), custom_call_target="tpu_custom_call" | custom-call | flops 362387872 | bytes 1800000 | tf_op jit(solution)/shard_map/pallas_call | solution.py:269
  90.7 11.4 %shard_map.208 = (bf16[256,1536]{1,0:T(8,128)(2,1)}, bf16[128,1536]{1,0:T(8,128)(2,1)}, bf16[128,1536]{1,0:T(8,128)(2,1)}, bf16[2,512,256]{2,1,0:T(8,128)(2,1)}, f32[2,2,512,1]{3,2,1,0:T(8,128)}) custom-call(s32[1]{0:T(128)} %bitcast.y_ref.refs_0_, bf16[2,512,384]{2,1,0:T(8,128)(2,1)} %get-tuple-element.166.qkv.refs_1_, bf16[512,384]{1,0:T(8,128)(2,1)} %copy-done.58, ...), custom_call_target="tpu_custom_call" | custom-call | flops 1500000000 | bytes 2100000 | tf_op jit(solution)/shard_map/pallas_call | solution.py:348
  110.7 3.5 collective-permute-done.19
  116.2 5.0 collective-permute-done.12.refs_8_
  122.0 5.6 %collective-permute-done.13.refs_9_ = bf16[128,1536]{1,0:T(8,128)(2,1)S(1)} collective-permute-done((bf16[128,1536]{1,0:T(8,128)(2,1)S(1)}, bf16[128,1536]{1,0:T(8,128)(2,1)S(1)}, u32[]{:S(2)}, u32[]{:S(2)}) %collective-permute-start.13) | collective-permute-done | bytes 393248 | tf_op jit(solution)/shard_map/ppermute | solution.py:32
  128.4 11.3 %shard_map.207 = (bf16[256,1536]{1,0:T(8,128)(2,1)}, bf16[256,1536]{1,0:T(8,128)(2,1)}, bf16[2,512,256]{2,1,0:T(8,128)(2,1)}, f32[2,2,512,1]{3,2,1,0:T(8,128)}) custom-call(s32[1]{0:T(128)} %bitcast.y_ref.refs_0_, bf16[2,512,384]{2,1,0:T(8,128)(2,1)} %get-tuple-element.153.qkv.refs_1_, bf16[512,384]{1,0:T(8,128)(2,1)} %copy-done.59, ...), custom_call_target="tpu_custom_call" | custom-call | flops 1500000000 | bytes 2100000 | tf_op jit(solution)/shard_map/pallas_call | solution.py:348
  144.2 14.2 %collective-permute-done.23.refs_12_.refs_2_ = bf16[576,1024]{1,0:T(8,128)(2,1)} collective-permute-done((bf16[576,1024]{1,0:T(8,128)(2,1)S(1)}, bf16[576,1024]{1,0:T(8,128)(2,1)}, u32[]{:S(2)}, u32[]{:S(2)}) %collective-permute-start.23) | collective-permute-done | bytes 1179680 | tf_op jit(solution)/shard_map/ppermute | solution.py:32
  164.9 14.5 %collective-permute-done.26.refs_2_ = bf16[256,1536]{1,0:T(8,128)(2,1)S(1)} collective-permute-done((bf16[256,1536]{1,0:T(8,128)(2,1)S(1)}, bf16[256,1536]{1,0:T(8,128)(2,1)S(1)}, u32[]{:S(2)}, u32[]{:S(2)}) %collective-permute-start.26) | collective-permute-done | bytes 786464 | tf_op jit(solution)/shard_map/ppermute | solution.py:32
  179.4 4.0 collective-permute-done.29.refs_13_.refs_3_
  185.4 9.6 %collective-permute-done.27.refs_3_ = bf16[128,1536]{1,0:T(8,128)(2,1)S(1)} collective-permute-done((bf16[128,1536]{1,0:T(8,128)(2,1)S(1)}, bf16[128,1536]{1,0:T(8,128)(2,1)S(1)}, u32[]{:S(2)}, u32[]{:S(2)}) %collective-permute-start.27) | collective-permute-done | bytes 393248 | tf_op jit(solution)/shard_map/ppermute | solution.py:32
  196.1 27.2 %shard_map.209 = (bf16[2,1024,512]{2,1,0:T(8,128)(2,1)}, bf16[2,1024,1024]{2,1,0:T(8,128)(2,1)}, bf16[256,1536]{1,0:T(8,128)(2,1)}, bf16[256,1536]{1,0:T(8,128)(...) custom-call(s32[1]{0:T(128)} %bitcast.6.z_ref, ...), custom_call_target="tpu_custom_call" | custom-call | flops 4831838208 | bytes 7500000 | tf_op jit(solution)/shard_map/pallas_call | solution.py:491
  223.3 7.1 %shard_map.212 = bf16[1536,1024]{1,0:T(8,128)(2,1)} custom-call(bf16[1024,1536]{1,0:T(8,128)(2,1)} %get-tuple-element.185.left, bf16[2,1024,1024]{2,1,0:T(8,128)(2,1)} %get-tuple-element.186.right), custom_call_target="tpu_custom_call" | custom-call | flops 966367616 | bytes 3000000 | tf_op jit(solution)/shard_map/pallas_call | solution.py:611
  234.1 5.2 %shard_map.211 = bf16[512,1536]{1,0:T(8,128)(2,1)} custom-call(bf16[2,1024,512]{2,1,0:T(8,128)(2,1)} %get-tuple-element.174.hidden.left, bf16[1024,1536]{1,0:T(8,128)(2,1)} %get-tuple-element.184.right), custom_call_target="tpu_custom_call" | custom-call | flops 483183808 | bytes 3000000 | tf_op jit(solution)/shard_map/pallas_call | solution.py:611
  239.3 7.9 %shard_map.213 = bf16[1536,1024]{1,0:T(8,128)(2,1)} custom-call(bf16[1024,1536]{1,0:T(8,128)(2,1)} %get-tuple-element.185.left, bf16[2,1024,1024]{2,1,0:T(8,128)(2,1)} %get-tuple-element.186.right, bf16[1536,1024]{1,0:T(8,128)(2,1)} %collective-permute-done.36.rest_0_), custom_call_target="tpu_custom_call" | custom-call | flops 966367616 | bytes 3000000 | tf_op jit(solution)/shard_map/pallas_call | solution.py:611
  251.8 4.8 all-to-all-start.1
  256.5 12.5 %collective-permute-done.37 = bf16[256,1536]{1,0:T(8,128)(2,1)S(1)} collective-permute-done((bf16[256,1536]{1,0:T(8,128)(2,1)}, bf16[256,1536]{1,0:T(8,128)(2,1)S(1)}, u32[]{:S(2)}, u32[]{:S(2)}) %collective-permute-start.37) | collective-permute-done | bytes 786464 | tf_op jit(solution)/shard_map/ppermute | solution.py:32
  272.4 3.2 fusion.24
  277.3 9.0 %shard_map.210 = (bf16[256,1536]{1,0:T(8,128)(2,1)}, bf16[256,1536]{1,0:T(8,128)(2,1)}, bf16[256,1536]{1,0:T(8,128)(2,1)}, bf16[128,1536]{1,0:T(8,128)(2,1)}, bf16[128,1536]{1,0:T(8,128)(2,1)}) custom-call(s32[1]{0:T(128)} %bitcast.6.z_ref, bf16[2,1024,512]{2,1,0:T(8,128)(2,1)} %get-tuple-element.174.hidden.left, ...), custom_call_target="tpu_custom_call" | custom-call | flops 966367616 | bytes 2400000 | tf_op jit(solution)/shard_map/pallas_call | solution.py:573
  286.3 5.7 %shard_map.214 = bf16[512,1536]{1,0:T(8,128)(2,1)} custom-call(bf16[2,1024,512]{2,1,0:T(8,128)(2,1)} %get-tuple-element.174.hidden.left, bf16[1024,1536]{1,0:T(8,128)(2,1)} %get-tuple-element.184.right, bf16[512,1536]{1,0:T(8,128)(2,1)} %collective-permute-done.41.rest_0_), custom_call_target="tpu_custom_call" | custom-call | flops 483183808 | bytes 3000000 | tf_op jit(solution)/shard_map/pallas_call | solution.py:611
  298.3 17.0 %shard_map.215 = (bf16[2,512,384]{2,1,0:T(8,128)(2,1)}, f32[2,512,256]{2,1,0:T(8,128)}, bf16[512,384]{1,0:T(8,128)(2,1)}, bf16[2,192,1536]{2,1,0:T(8,128)(2,1)}) custom-call(s32[1]{0:T(128)} %bitcast.y_ref.refs_0_, bf16[2,512,384]{2,1,0:T(8,128)(2,1)} %get-tuple-element.153.qkv.refs_1_, bf16[512,384]{1,0:T(8,128)(2,1)} %copy-done.59, ...), custom_call_target="tpu_custom_call" | custom-call | flops 3600000000 | bytes 3000000 | tf_op jit(solution)/shard_map/pallas_call | solution.py:744
  317.3 17.5 %shard_map.216 = (bf16[2,512,384]{2,1,0:T(8,128)(2,1)}, f32[2,512,256]{2,1,0:T(8,128)}, bf16[512,384]{1,0:T(8,128)(2,1)}, bf16[2,192,1536]{2,1,0:T(8,128)(2,1)}) custom-call(s32[1]{0:T(128)} %bitcast.y_ref.refs_0_, bf16[2,512,384]{2,1,0:T(8,128)(2,1)} %get-tuple-element.166.qkv.refs_1_, bf16[512,384]{1,0:T(8,128)(2,1)} %copy-done.58, ...), custom_call_target="tpu_custom_call" | custom-call | flops 3600000000 | bytes 3000000 | tf_op jit(solution)/shard_map/pallas_call | solution.py:744
  352.3 7.0 %collective-permute-done.49.grad_halo = bf16[512,384]{1,0:T(8,128)(2,1)} collective-permute-done((bf16[512,384]{1,0:T(8,128)(2,1)}, bf16[512,384]{1,0:T(8,128)(2,1)}, u32[]{:S(2)}, u32[]{:S(2)}) %collective-permute-start.49) | collective-permute-done | bytes 393248 | tf_op jit(solution)/shard_map/ppermute | solution.py:32
  359.3 4.6 all-to-all-start.3
  363.9 7.0 %shard_map.218 = (bf16[2,512,384]{2,1,0:T(8,128)(2,1)}, bf16[256,1536]{1,0:T(8,128)(2,1)}, bf16[128,1536]{1,0:T(8,128)(2,1)}, bf16[128,1536]{1,0:T(8,128)(2,1)}) custom-call(bf16[2,512,384]{2,1,0:T(8,128)(2,1)} %get-tuple-element.213.grad_query, f32[2,512,256]{2,1,0:T(8,128)} %get-tuple-element.214.grad_kv, ...), custom_call_target="tpu_custom_call" | custom-call | flops 362387872 | bytes 1800000 | tf_op jit(solution)/shard_map/pallas_call | solution.py:816
  370.8 3.4 fusion.6
  374.3 6.9 %shard_map.217 = (bf16[2,512,384]{2,1,0:T(8,128)(2,1)}, bf16[256,1536]{1,0:T(8,128)(2,1)}, bf16[256,1536]{1,0:T(8,128)(2,1)}) custom-call(bf16[2,512,384]{2,1,0:T(8,128)(2,1)} %get-tuple-element.209.grad_query, f32[2,512,256]{2,1,0:T(8,128)} %get-tuple-element.210.grad_kv, bf16[512,384]{1,0:T(8,128)(2,1)} %collective-permute-done.48.grad_halo, ...), custom_call_target="tpu_custom_call" | custom-call | flops 362387872 | bytes 1800000 | tf_op jit(solution)/shard_map/pallas_call | solution.py:816
  381.2 3.3 fusion.1
  397.1 3.8 all-to-all-start.2
  406.4 11.9 %collective-permute-done.51 = bf16[128,1536]{1,0:T(8,128)(2,1)S(1)} collective-permute-done((bf16[128,1536]{1,0:T(8,128)(2,1)}, bf16[128,1536]{1,0:T(8,128)(2,1)S(1)}, u32[]{:S(2)}, u32[]{:S(2)}) %collective-permute-start.51) | collective-permute-done | bytes 393248 | tf_op jit(solution)/shard_map/ppermute | solution.py:32
  426.7 7.0 %collective-permute-done.61 = bf16[384,1024]{1,0:T(8,128)(2,1)} collective-permute-done((bf16[384,1024]{1,0:T(8,128)(2,1)}, bf16[384,1024]{1,0:T(8,128)(2,1)}, u32[]{:S(2)}, u32[]{:S(2)}) %collective-permute-start.61) | collective-permute-done | bytes 786464 | tf_op jit(solution)/shard_map/ppermute | solution.py:32
  437.4 4.0 all-to-all-done.2
  443.5 7.1 %collective-permute-done.53 = bf16[256,1536]{1,0:T(8,128)(2,1)} collective-permute-done((bf16[256,1536]{1,0:T(8,128)(2,1)}, bf16[256,1536]{1,0:T(8,128)(2,1)}, u32[]{:S(2)}, u32[]{:S(2)}) %collective-permute-start.53) | collective-permute-done | bytes 786464 | tf_op jit(solution)/shard_map/ppermute | solution.py:32
  453.7 4.0 collective-permute-done.64.b2
  460.3 13.8 %collective-permute-start.59 = (bf16[576,384]{1,0:T(8,128)(2,1)}, bf16[576,384]{1,0:T(8,128)(2,1)}, u32[]{:S(2)}, u32[]{:S(2)}) collective-permute-start(bf16[576,384]{1,0:T(8,128)(2,1)} %pad_maximum_fusion.11.refs_0_), channel_id=1, source_target_pairs={{0,16},{1,17},{2,18},{3,19},{4,20},{5,21},{6,22},{7,23},{8,24},{9,... | collective-permute-start | bytes 1327112 | tf_op jit(solution)/shard_map/ppermute | solution.py:32
  474.1 6.5 %shard_map.219 = (f32[192,4096]{1,0:T(8,128)}, f32[192,4096]{1,0:T(8,128)}, f32[192,1]{1,0:T(8,128)}) custom-call(s32[1]{0:T(128)} %bitcast.1.d_ref, bf16[2,192,1024]{2,1,0:T(8,128)(2,1)} %pad_maximum_fusion.7.refs_0_, bf16[2,192,1024]{2,1,0:T(8,128)(2,1)} %bitcast.40.refs_1_, bf16[2,192,1024]{2,1,0:T(8,128)(2,1)} %bitcast.41.refs_2_, ...), custom_call_target="tpu_custom_call" | custom-call | flops 1415577 | bytes 3774873 | tf_op jit(solution)/shard_map/pallas_call | solution.py:848
  481.4 3.3 shard_map.220
  485.2 3.2 fusion.4
  489.1 5.2 %shard_map.221 = (f32[192,1536]{1,0:T(8,128)}, f32[192,768]{1,0:T(8,128)}, f32[192,768]{1,0:T(8,128)}, f32[192,1536]{1,0:T(8,128)}, f32[192,1]{1,0:T(8,128)}) custom-call(s32[1]{0:T(128)} %bitcast.1.d_ref, bf16[576,384]{1,0:T(8,128)(2,1)} %pad_maximum_fusion.11.refs_0_, bf16[576,384]{1,0:T(8,128)(2,1)} %collective-permute-done.58.refs_1_, ...), custom_call_target="tpu_custom_call" | custom-call | flops 1200000000 | bytes 2400000 | tf_op jit(solution)/shard_map/pallas_call | solution.py:927
  (382 shorter events, 145.2 us)
Async XLA Ops:
  0.7 43.2 %collective-permute-start.3 = (s32[1,8]{1,0:T(1,128)}, s32[1,8]{1,0:T(1,128)S(1)}, u32[]{:S(2)}, u32[]{:S(2)}) collective-permute-start(s32[1,8]{1,0:T(1,128)} %param.21), channel_id=1, source_target_pairs={{0,16},{1,17},{2,18},{3,19},{4,20},{5,21},{6,22},{7,23},{8,24},{9,... | collective-permute-start | bytes 104 | tf_op jit(solution)/shard_map/ppermute | solution.py:32
  9.2 19.0 %collective-permute-start.4 = (bf16[256,1536]{1,0:T(8,128)(2,1)}, bf16[256,1536]{1,0:T(8,128)(2,1)}, u32[]{:S(2)}, u32[]{:S(2)}) collective-permute-start(bf16[256,1536]{1,0:T(8,128)(2,1)} %refs_0_.1), channel_id=1, source_target_pairs={{0,16},{1,17},{2,18},{3,19},{4,20},{5,21},{6,22},{7,23},{8,24},{9,... | collective-permute-start | bytes 2359304 | tf_op jit(solution)/shard_map/ppermute | solution.py:32
  13.5 24.6 %collective-permute-start.1 = (bf16[256,1536]{1,0:T(8,128)(2,1)S(1)}, bf16[256,1536]{1,0:T(8,128)(2,1)}, u32[]{:S(2)}, u32[]{:S(2)}) collective-permute-start(bf16[256,1536]{1,0:T(8,128)(2,1)S(1)} %copy-done.5), channel_id=1, source_target_pairs={{0,1},{1,0},{2,3},{3,2},{4,5},{5,4},{6,7},{7,6},{8,9},{9,8},{10,11... | collective-permute-start | bytes 2359304 | tf_op jit(solution)/shard_map/ppermute | solution.py:32
  16.3 40.1 %all-to-all-start = ((bf16[4,400,384]{2,1,0:T(8,128)(2,1)}), bf16[4,400,384]{2,1,0:T(8,128)(2,1)S(1)}, u32[]{:S(2)}, u32[]{:S(2)}) async-start(bf16[4,400,384]{2,1,0:T(8,128)(2,1)} %broadcast_in_dim.66), calls=%async_computation | async-start | bytes 2457600 | tf_op jit(solution)/shard_map/all_to_all | solution.py:100
  32.1 24.3 %collective-permute-start.6 = (bf16[48,1536]{1,0:T(8,128)(2,1)}, bf16[48,1536]{1,0:T(8,128)(2,1)}, u32[]{:S(2)}, u32[]{:S(2)}) collective-permute-start(bf16[48,1536]{1,0:T(8,128)(2,1)} %constant_dynamic-slice_fusion.3), channel_id=1, source_target_pairs={{0,0},{1,1},{2,8},{3,9},{4,16},{5,17},{6,24},{7,25},{8,2},{9,3},{1... | collective-permute-start | bytes 442376 | tf_op jit(solution)/shard_map/ppermute | solution.py:32
  39.1 17.2 %collective-permute-start.7 = (bf16[128,1536]{1,0:T(8,128)(2,1)S(1)}, bf16[128,1536]{1,0:T(8,128)(2,1)S(1)}, u32[]{:S(2)}, u32[]{:S(2)}) collective-permute-start(bf16[128,1536]{1,0:T(8,128)(2,1)S(1)} %slice.390), channel_id=1, source_target_pairs={{0,16},{1,17},{2,18},{3,19},{4,20},{5,21},{6,22},{7,23},{8,24},{9,... | collective-permute-start | bytes 1179656 | tf_op jit(solution)/shard_map/ppermute | solution.py:32
  57.2 19.3 %collective-permute-start.16 = (bf16[48,1536]{1,0:T(8,128)(2,1)}, bf16[48,1536]{1,0:T(8,128)(2,1)S(1)}, u32[]{:S(2)}, u32[]{:S(2)}) collective-permute-start(bf16[48,1536]{1,0:T(8,128)(2,1)} %collective-permute-done.6), channel_id=1, source_target_pairs={{0,6},{1,7},{2,4},{3,5},{4,2},{5,3},{6,0},{7,1},{8,14},{9,15},{10,... | collective-permute-start | bytes 442376 | tf_op jit(solution)/shard_map/ppermute | solution.py:32
  57.2 19.2 %collective-permute-start.15 = (bf16[48,1536]{1,0:T(8,128)(2,1)}, bf16[48,1536]{1,0:T(8,128)(2,1)S(1)}, u32[]{:S(2)}, u32[]{:S(2)}) collective-permute-start(bf16[48,1536]{1,0:T(8,128)(2,1)} %collective-permute-done.6), channel_id=1, source_target_pairs={{0,4},{1,5},{2,6},{3,7},{4,0},{5,1},{6,2},{7,3},{8,12},{9,13},{10,... | collective-permute-start | bytes 442376 | tf_op jit(solution)/shard_map/ppermute | solution.py:32
  57.3 19.1 %collective-permute-start.14 = (bf16[48,1536]{1,0:T(8,128)(2,1)}, bf16[48,1536]{1,0:T(8,128)(2,1)S(1)}, u32[]{:S(2)}, u32[]{:S(2)}) collective-permute-start(bf16[48,1536]{1,0:T(8,128)(2,1)} %collective-permute-done.6), channel_id=1, source_target_pairs={{0,2},{1,3},{2,0},{3,1},{4,6},{5,7},{6,4},{7,5},{8,10},{9,11},{10,... | collective-permute-start | bytes 442376 | tf_op jit(solution)/shard_map/ppermute | solution.py:32
  79.6 27.3 %collective-permute-start.11 = (bf16[256,1536]{1,0:T(8,128)(2,1)S(1)}, bf16[256,1536]{1,0:T(8,128)(2,1)}, u32[]{:S(2)}, u32[]{:S(2)}) collective-permute-start(bf16[256,1536]{1,0:T(8,128)(2,1)S(1)} %copy-done.23), channel_id=1, source_target_pairs={{0,1},{1,0},{2,3},{3,2},{4,5},{5,4},{6,7},{7,6},{8,9},{9,8},{10,11... | collective-permute-start | bytes 2359304 | tf_op jit(solution)/shard_map/ppermute | solution.py:32
  81.2 26.9 %collective-permute-start.10 = (bf16[256,1536]{1,0:T(8,128)(2,1)S(1)}, bf16[256,1536]{1,0:T(8,128)(2,1)}, u32[]{:S(2)}, u32[]{:S(2)}) collective-permute-start(bf16[256,1536]{1,0:T(8,128)(2,1)S(1)} %copy-done.23), channel_id=1, source_target_pairs={{0,16},{1,17},{2,18},{3,19},{4,20},{5,21},{6,22},{7,23},{8,24},{9,... | collective-permute-start | bytes 2359304 | tf_op jit(solution)/shard_map/ppermute | solution.py:32
  84.1 18.6 %collective-permute-start.9 = (bf16[512,384]{1,0:T(8,128)(2,1)}, bf16[512,384]{1,0:T(8,128)(2,1)S(1)}, u32[]{:S(2)}, u32[]{:S(2)}) collective-permute-start(bf16[512,384]{1,0:T(8,128)(2,1)} %get-tuple-element.154), channel_id=1, source_target_pairs={{0,2},{1,3},{2,4},{3,5},{4,6},{5,7},{8,10},{9,11},{10,12},{11,13},... | collective-permute-start | bytes 1179656 | tf_op jit(solution)/shard_map/ppermute | solution.py:32
  102.7 55.7 %collective-permute-start.24 = (bf16[576,1024]{1,0:T(8,128)(2,1)S(1)}, bf16[576,1024]{1,0:T(8,128)(2,1)S(1)}, u32[]{:S(2)}, u32[]{:S(2)}) collective-permute-start(bf16[576,1024]{1,0:T(8,128)(2,1)S(1)} %copy-done.10), channel_id=1, source_target_pairs={{0,2},{1,3},{2,0},{3,1},{4,6},{5,7},{6,4},{7,5},{8,10},{9,11},{10,... | collective-permute-start | bytes 3538952 | tf_op jit(solution)/shard_map/ppermute | solution.py:32
  105.2 53.1 %collective-permute-start.23 = (bf16[576,1024]{1,0:T(8,128)(2,1)S(1)}, bf16[576,1024]{1,0:T(8,128)(2,1)}, u32[]{:S(2)}, u32[]{:S(2)}) collective-permute-start(bf16[576,1024]{1,0:T(8,128)(2,1)S(1)} %copy-done.10), channel_id=1, source_target_pairs={{0,4},{1,5},{2,6},{3,7},{4,0},{5,1},{6,2},{7,3},{8,12},{9,13},{10,... | collective-permute-start | bytes 3538952 | tf_op jit(solution)/shard_map/ppermute | solution.py:32
  106.9 32.8 %collective-permute-start.21 = (bf16[128,1536]{1,0:T(8,128)(2,1)}, bf16[128,1536]{1,0:T(8,128)(2,1)S(1)}, u32[]{:S(2)}, u32[]{:S(2)}) collective-permute-start(bf16[128,1536]{1,0:T(8,128)(2,1)} %get-tuple-element.170), channel_id=1, source_target_pairs={{0,16},{1,17},{2,18},{3,19},{4,20},{5,21},{6,22},{7,23},{8,24},{9,... | collective-permute-start | bytes 1179656 | tf_op jit(solution)/shard_map/ppermute | solution.py:32
  121.1 37.3 %collective-permute-start.20 = (bf16[256,1536]{1,0:T(8,128)(2,1)}, bf16[256,1536]{1,0:T(8,128)(2,1)}, u32[]{:S(2)}, u32[]{:S(2)}) collective-permute-start(bf16[256,1536]{1,0:T(8,128)(2,1)} %pad_maximum_fusion.1), channel_id=1, source_target_pairs={{0,16},{1,17},{2,18},{3,19},{4,20},{5,21},{6,22},{7,23},{8,24},{9,... | collective-permute-start | bytes 2359304 | tf_op jit(solution)/shard_map/ppermute | solution.py:32
  158.4 24.9 %collective-permute-start.29 = (bf16[576,1024]{1,0:T(8,128)(2,1)}, bf16[576,1024]{1,0:T(8,128)(2,1)S(1)}, u32[]{:S(2)}, u32[]{:S(2)}) collective-permute-start(bf16[576,1024]{1,0:T(8,128)(2,1)} %collective-permute-done.23.refs_12_.refs_2_), channel_id=1, source_target_pairs={{0,2},{1,3},{2,0},{3,1},{4,6},{5,7},{6,4},{7,5},{8,10},{9,11},{10,... | collective-permute-start | bytes 3538952 | tf_op jit(solution)/shard_map/ppermute | solution.py:32
  162.7 16.6 %collective-permute-start.26 = (bf16[256,1536]{1,0:T(8,128)(2,1)S(1)}, bf16[256,1536]{1,0:T(8,128)(2,1)S(1)}, u32[]{:S(2)}, u32[]{:S(2)}) collective-permute-start(bf16[256,1536]{1,0:T(8,128)(2,1)S(1)} %multiply_convert_fusion.refs_0_), channel_id=1, source_target_pairs={{0,16},{1,17},{2,18},{3,19},{4,20},{5,21},{6,22},{7,23},{8,24},{9,... | collective-permute-start | bytes 2359304 | tf_op jit(solution)/shard_map/ppermute | solution.py:32
  163.9 20.5 %collective-permute-start.30 = (bf16[576,1024]{1,0:T(8,128)(2,1)S(1)}, bf16[576,1024]{1,0:T(8,128)(2,1)S(1)}, u32[]{:S(2)}, u32[]{:S(2)}) collective-permute-start(bf16[576,1024]{1,0:T(8,128)(2,1)S(1)} %copy-done.10), channel_id=1, source_target_pairs={{0,8},{1,9},{2,10},{3,11},{4,12},{5,13},{6,14},{7,15},{8,0},{9,1},... | collective-permute-start | bytes 3538952 | tf_op jit(solution)/shard_map/ppermute | solution.py:32
  163.9 21.5 %collective-permute-start.31 = (bf16[576,1024]{1,0:T(8,128)(2,1)S(1)}, bf16[576,1024]{1,0:T(8,128)(2,1)S(1)}, u32[]{:S(2)}, u32[]{:S(2)}) collective-permute-start(bf16[576,1024]{1,0:T(8,128)(2,1)S(1)} %copy-done.18), channel_id=1, source_target_pairs={{0,8},{1,9},{2,10},{3,11},{4,12},{5,13},{6,14},{7,15},{8,0},{9,1},... | collective-permute-start | bytes 3538952 | tf_op jit(solution)/shard_map/ppermute | solution.py:32
  164.4 19.4 %collective-permute-start.25 = (bf16[256,1536]{1,0:T(8,128)(2,1)S(1)}, bf16[256,1536]{1,0:T(8,128)(2,1)S(1)}, u32[]{:S(2)}, u32[]{:S(2)}) collective-permute-start(bf16[256,1536]{1,0:T(8,128)(2,1)S(1)} %multiply_convert_fusion.refs_0_), channel_id=1, source_target_pairs={{0,1},{1,0},{2,3},{3,2},{4,5},{5,4},{6,7},{7,6},{8,9},{9,8},{10,11... | collective-permute-start | bytes 2359304 | tf_op jit(solution)/shard_map/ppermute | solution.py:32
  230.4 16.8 %collective-permute-start.34 = (bf16[128,1536]{1,0:T(8,128)(2,1)}, bf16[128,1536]{1,0:T(8,128)(2,1)S(1)}, u32[]{:S(2)}, u32[]{:S(2)}) collective-permute-start(bf16[128,1536]{1,0:T(8,128)(2,1)} %get-tuple-element.182), channel_id=1, source_target_pairs={{0,1},{1,0},{2,3},{3,2},{4,5},{5,4},{6,7},{7,6},{8,9},{9,8},{10,11... | collective-permute-start | bytes 1179656 | tf_op jit(solution)/shard_map/ppermute | solution.py:32
  249.4 19.6 %collective-permute-start.37 = (bf16[256,1536]{1,0:T(8,128)(2,1)}, bf16[256,1536]{1,0:T(8,128)(2,1)S(1)}, u32[]{:S(2)}, u32[]{:S(2)}) collective-permute-start(bf16[256,1536]{1,0:T(8,128)(2,1)} %pad_maximum_fusion.3), channel_id=1, source_target_pairs={{0,16},{1,17},{2,18},{3,19},{4,20},{5,21},{6,22},{7,23},{8,24},{9,... | collective-permute-start | bytes 2359304 | tf_op jit(solution)/shard_map/ppermute | solution.py:32
  251.3 19.4 %collective-permute-start.38 = (bf16[256,1536]{1,0:T(8,128)(2,1)}, bf16[256,1536]{1,0:T(8,128)(2,1)}, u32[]{:S(2)}, u32[]{:S(2)}) collective-permute-start(bf16[256,1536]{1,0:T(8,128)(2,1)} %pad_maximum_fusion.4), channel_id=1, source_target_pairs={{0,1},{1,0},{2,3},{3,2},{4,5},{5,4},{6,7},{7,6},{8,9},{9,8},{10,11... | collective-permute-start | bytes 2359304 | tf_op jit(solution)/shard_map/ppermute | solution.py:32
  251.7 34.5 %collective-permute-start.41 = (bf16[512,1536]{1,0:T(8,128)(2,1)}, bf16[512,1536]{1,0:T(8,128)(2,1)}, u32[]{:S(2)}, u32[]{:S(2)}) collective-permute-start(bf16[512,1536]{1,0:T(8,128)(2,1)} %shard_map.211), channel_id=1, source_target_pairs={{0,8},{1,9},{2,10},{3,11},{4,12},{5,13},{6,14},{7,15},{8,0},{9,1},... | collective-permute-start | bytes 4718600 | tf_op jit(solution)/shard_map/ppermute | solution.py:32
  251.8 88.7 %all-to-all-start.1 = ((bf16[4,384,1024]{2,1,0:T(8,128)(2,1)}), bf16[4,384,1024]{2,1,0:T(8,128)(2,1)}, u32[]{:S(2)}, u32[]{:S(2)}) async-start(bf16[4,384,1024]{2,1,0:T(8,128)(2,1)} %bitcast.86), calls=%async_computation.1 | async-start | bytes 6291456 | tf_op jit(solution)/shard_map/all_to_all | solution.py:100
  275.7 18.4 %collective-permute-start.40 = (bf16[256,1536]{1,0:T(8,128)(2,1)}, bf16[256,1536]{1,0:T(8,128)(2,1)S(1)}, u32[]{:S(2)}, u32[]{:S(2)}) collective-permute-start(bf16[256,1536]{1,0:T(8,128)(2,1)} %get-tuple-element.190.refs_10_), channel_id=1, source_target_pairs={{0,1},{1,0},{2,3},{3,2},{4,5},{5,4},{6,7},{7,6},{8,9},{9,8},{10,11... | collective-permute-start | bytes 2359304 | tf_op jit(solution)/shard_map/ppermute | solution.py:32
  276.2 18.1 %collective-permute-start.39 = (bf16[256,1536]{1,0:T(8,128)(2,1)}, bf16[256,1536]{1,0:T(8,128)(2,1)S(1)}, u32[]{:S(2)}, u32[]{:S(2)}) collective-permute-start(bf16[256,1536]{1,0:T(8,128)(2,1)} %get-tuple-element.190.refs_10_), channel_id=1, source_target_pairs={{0,16},{1,17},{2,18},{3,19},{4,20},{5,21},{6,22},{7,23},{8,24},{9,... | collective-permute-start | bytes 2359304 | tf_op jit(solution)/shard_map/ppermute | solution.py:32
  296.1 19.3 %collective-permute-start.42 = (bf16[128,1536]{1,0:T(8,128)(2,1)S(1)}, bf16[128,1536]{1,0:T(8,128)(2,1)S(1)}, u32[]{:S(2)}, u32[]{:S(2)}) collective-permute-start(bf16[128,1536]{1,0:T(8,128)(2,1)S(1)} %slice.329), channel_id=1, source_target_pairs={{0,1},{1,0},{2,3},{3,2},{4,5},{5,4},{6,7},{7,6},{8,9},{9,8},{10,11... | collective-permute-start | bytes 1179656 | tf_op jit(solution)/shard_map/ppermute | solution.py:32
  297.2 18.1 %collective-permute-start.43 = (bf16[128,1536]{1,0:T(8,128)(2,1)S(1)}, bf16[128,1536]{1,0:T(8,128)(2,1)}, u32[]{:S(2)}, u32[]{:S(2)}) collective-permute-start(bf16[128,1536]{1,0:T(8,128)(2,1)S(1)} %slice.330), channel_id=1, source_target_pairs={{0,16},{1,17},{2,18},{3,19},{4,20},{5,21},{6,22},{7,23},{8,24},{9,... | collective-permute-start | bytes 1179656 | tf_op jit(solution)/shard_map/ppermute | solution.py:32
  315.4 29.6 %collective-permute-start.44 = (bf16[128,1536]{1,0:T(8,128)(2,1)}, bf16[128,1536]{1,0:T(8,128)(2,1)}, u32[]{:S(2)}, u32[]{:S(2)}) collective-permute-start(bf16[128,1536]{1,0:T(8,128)(2,1)} %get-tuple-element.202), channel_id=1, source_target_pairs={{0,1},{1,0},{2,3},{3,2},{4,5},{5,4},{6,7},{7,6},{8,9},{9,8},{10,11... | collective-permute-start | bytes 1179656 | tf_op jit(solution)/shard_map/ppermute | solution.py:32
  316.4 28.6 %collective-permute-start.45 = (bf16[128,1536]{1,0:T(8,128)(2,1)}, bf16[128,1536]{1,0:T(8,128)(2,1)}, u32[]{:S(2)}, u32[]{:S(2)}) collective-permute-start(bf16[128,1536]{1,0:T(8,128)(2,1)} %get-tuple-element.203), channel_id=1, source_target_pairs={{0,16},{1,17},{2,18},{3,19},{4,20},{5,21},{6,22},{7,23},{8,24},{9,... | collective-permute-start | bytes 1179656 | tf_op jit(solution)/shard_map/ppermute | solution.py:32
  347.8 26.5 %collective-permute-start.48 = (bf16[512,384]{1,0:T(8,128)(2,1)}, bf16[512,384]{1,0:T(8,128)(2,1)}, u32[]{:S(2)}, u32[]{:S(2)}) collective-permute-start(bf16[512,384]{1,0:T(8,128)(2,1)} %get-tuple-element.211), channel_id=1, source_target_pairs={{2,0},{3,1},{4,2},{5,3},{6,4},{7,5},{10,8},{11,9},{12,10},{13,11},... | collective-permute-start | bytes 1179656 | tf_op jit(solution)/shard_map/ppermute | solution.py:32
  359.3 37.8 %all-to-all-start.3 = ((bf16[4,128,1536]{2,1,0:T(8,128)(2,1)}), bf16[4,128,1536]{2,1,0:T(8,128)(2,1)}, u32[]{:S(2)}, u32[]{:S(2)}) async-start(bf16[4,128,1536]{2,1,0:T(8,128)(2,1)} %bitcast.44), calls=%async_computation.3 | async-start | bytes 3145728 | tf_op jit(solution)/shard_map/all_to_all | solution.py:100
  387.7 30.6 %collective-permute-start.46 = (bf16[256,1536]{1,0:T(8,128)(2,1)}, bf16[256,1536]{1,0:T(8,128)(2,1)}, u32[]{:S(2)}, u32[]{:S(2)}) collective-permute-start(bf16[256,1536]{1,0:T(8,128)(2,1)} %pad_maximum_fusion.5), channel_id=1, source_target_pairs={{0,16},{1,17},{2,18},{3,19},{4,20},{5,21},{6,22},{7,23},{8,24},{9,... | collective-permute-start | bytes 2359304 | tf_op jit(solution)/shard_map/ppermute | solution.py:32
  390.8 27.5 %collective-permute-start.47 = (bf16[256,1536]{1,0:T(8,128)(2,1)}, bf16[256,1536]{1,0:T(8,128)(2,1)}, u32[]{:S(2)}, u32[]{:S(2)}) collective-permute-start(bf16[256,1536]{1,0:T(8,128)(2,1)} %pad_maximum_fusion.6), channel_id=1, source_target_pairs={{0,1},{1,0},{2,3},{3,2},{4,5},{5,4},{6,7},{7,6},{8,9},{9,8},{10,11... | collective-permute-start | bytes 2359304 | tf_op jit(solution)/shard_map/ppermute | solution.py:32
  397.1 44.2 %all-to-all-start.2 = ((bf16[4,576,384]{2,1,0:T(8,128)(2,1)}), bf16[4,576,384]{2,1,0:T(8,128)(2,1)S(1)}, u32[]{:S(2)}, u32[]{:S(2)}) async-start(bf16[4,576,384]{2,1,0:T(8,128)(2,1)} %add_convert_fusion), calls=%async_computation.2 | async-start | bytes 3538944 | tf_op jit(solution)/shard_map/all_to_all | solution.py:100
  401.0 17.3 %collective-permute-start.51 = (bf16[128,1536]{1,0:T(8,128)(2,1)}, bf16[128,1536]{1,0:T(8,128)(2,1)S(1)}, u32[]{:S(2)}, u32[]{:S(2)}) collective-permute-start(bf16[128,1536]{1,0:T(8,128)(2,1)} %get-tuple-element.218), channel_id=1, source_target_pairs={{0,1},{1,0},{2,3},{3,2},{4,5},{5,4},{6,7},{7,6},{8,9},{9,8},{10,11... | collective-permute-start | bytes 1179656 | tf_op jit(solution)/shard_map/ppermute | solution.py:32
  402.3 16.0 %collective-permute-start.52 = (bf16[128,1536]{1,0:T(8,128)(2,1)}, bf16[128,1536]{1,0:T(8,128)(2,1)S(1)}, u32[]{:S(2)}, u32[]{:S(2)}) collective-permute-start(bf16[128,1536]{1,0:T(8,128)(2,1)} %get-tuple-element.219), channel_id=1, source_target_pairs={{0,16},{1,17},{2,18},{3,19},{4,20},{5,21},{6,22},{7,23},{8,24},{9,... | collective-permute-start | bytes 1179656 | tf_op jit(solution)/shard_map/ppermute | solution.py:32
  403.3 30.5 %collective-permute-start.61 = (bf16[384,1024]{1,0:T(8,128)(2,1)}, bf16[384,1024]{1,0:T(8,128)(2,1)}, u32[]{:S(2)}, u32[]{:S(2)}) collective-permute-start(bf16[384,1024]{1,0:T(8,128)(2,1)} %bitcast.89), channel_id=1, source_target_pairs={{0,16},{1,17},{2,18},{3,19},{4,20},{5,21},{6,22},{7,23},{8,24},{9,... | collective-permute-start | bytes 2359304 | tf_op jit(solution)/shard_map/ppermute | solution.py:32
  419.4 31.2 %collective-permute-start.53 = (bf16[256,1536]{1,0:T(8,128)(2,1)}, bf16[256,1536]{1,0:T(8,128)(2,1)}, u32[]{:S(2)}, u32[]{:S(2)}) collective-permute-start(bf16[256,1536]{1,0:T(8,128)(2,1)} %pad_maximum_fusion.8), channel_id=1, source_target_pairs={{0,16},{1,17},{2,18},{3,19},{4,20},{5,21},{6,22},{7,23},{8,24},{9,... | collective-permute-start | bytes 2359304 | tf_op jit(solution)/shard_map/ppermute | solution.py:32
  421.3 30.2 %collective-permute-start.54 = (bf16[256,1536]{1,0:T(8,128)(2,1)}, bf16[256,1536]{1,0:T(8,128)(2,1)}, u32[]{:S(2)}, u32[]{:S(2)}) collective-permute-start(bf16[256,1536]{1,0:T(8,128)(2,1)} %pad_maximum_fusion.9), channel_id=1, source_target_pairs={{0,1},{1,0},{2,3},{3,2},{4,5},{5,4},{6,7},{7,6},{8,9},{9,8},{10,11... | collective-permute-start | bytes 2359304 | tf_op jit(solution)/shard_map/ppermute | solution.py:32
  423.8 50.3 %collective-permute-start.60 = (bf16[384,1024]{1,0:T(8,128)(2,1)}, bf16[384,1024]{1,0:T(8,128)(2,1)}, u32[]{:S(2)}, u32[]{:S(2)}) collective-permute-start(bf16[384,1024]{1,0:T(8,128)(2,1)} %bitcast.90), channel_id=1, source_target_pairs={{0,8},{1,9},{2,10},{3,11},{4,12},{5,13},{6,14},{7,15},{8,0},{9,1},... | collective-permute-start | bytes 2359304 | tf_op jit(solution)/shard_map/ppermute | solution.py:32
  433.8 40.3 %collective-permute-start.62 = (bf16[384,1024]{1,0:T(8,128)(2,1)}, bf16[384,1024]{1,0:T(8,128)(2,1)}, u32[]{:S(2)}, u32[]{:S(2)}) collective-permute-start(bf16[384,1024]{1,0:T(8,128)(2,1)} %collective-permute-done.61), channel_id=1, source_target_pairs={{0,8},{1,9},{2,10},{3,11},{4,12},{5,13},{6,14},{7,15},{8,0},{9,1},... | collective-permute-start | bytes 2359304 | tf_op jit(solution)/shard_map/ppermute | solution.py:32
  436.3 21.4 %collective-permute-start.64 = (bf16[128,1536]{1,0:T(8,128)(2,1)}, bf16[128,1536]{1,0:T(8,128)(2,1)}, u32[]{:S(2)}, u32[]{:S(2)}) collective-permute-start(bf16[128,1536]{1,0:T(8,128)(2,1)} %reduce_sum.101.b0), channel_id=1, source_target_pairs={{0,16},{1,17},{2,18},{3,19},{4,20},{5,21},{6,22},{7,23},{8,24},{9,... | collective-permute-start | bytes 1179656 | tf_op jit(solution)/shard_map/ppermute | solution.py:32
  453.7 27.0 %collective-permute-start.63 = (bf16[128,1536]{1,0:T(8,128)(2,1)S(1)}, bf16[128,1536]{1,0:T(8,128)(2,1)S(1)}, u32[]{:S(2)}, u32[]{:S(2)}) collective-permute-start(bf16[128,1536]{1,0:T(8,128)(2,1)S(1)} %copy-done.15), channel_id=1, source_target_pairs={{0,8},{1,9},{2,10},{3,11},{4,12},{5,13},{6,14},{7,15},{8,0},{9,1},... | collective-permute-start | bytes 1179656 | tf_op jit(solution)/shard_map/ppermute | solution.py:32
  457.7 23.0 %collective-permute-start.65 = (bf16[128,1536]{1,0:T(8,128)(2,1)}, bf16[128,1536]{1,0:T(8,128)(2,1)}, u32[]{:S(2)}, u32[]{:S(2)}) collective-permute-start(bf16[128,1536]{1,0:T(8,128)(2,1)} %collective-permute-done.64.b2), channel_id=1, source_target_pairs={{0,8},{1,9},{2,10},{3,11},{4,12},{5,13},{6,14},{7,15},{8,0},{9,1},... | collective-permute-start | bytes 1179656 | tf_op jit(solution)/shard_map/ppermute | solution.py:32
  460.3 24.4 %collective-permute-start.59 = (bf16[576,384]{1,0:T(8,128)(2,1)}, bf16[576,384]{1,0:T(8,128)(2,1)}, u32[]{:S(2)}, u32[]{:S(2)}) collective-permute-start(bf16[576,384]{1,0:T(8,128)(2,1)} %pad_maximum_fusion.11.refs_0_), channel_id=1, source_target_pairs={{0,16},{1,17},{2,18},{3,19},{4,20},{5,21},{6,22},{7,23},{8,24},{9,... | collective-permute-start | bytes 1327112 | tf_op jit(solution)/shard_map/ppermute | solution.py:32
  (91 other events, 676.2 us)
